TPU v7x, 512 devices: a whole 4x8x8 slice. The times are simulated.
512 devices in a mesh: row: 16 (over x, z_hi, core), col: 32 (over z_lo, y).
Axes of the slice: x: 4, y: 8, z: 8 (z_hi: 2, z_lo: 4; z = z_hi * 4 + z_lo), core: 2. Of those that a mesh axis runs over, the one named last changes fastest.
Arguments:
- block_cols: int32 [512, 16], P(('row', 'col')), may hold values from 0 to 511, as said below
- blocks: bfloat16 [512, 16, 128, 128], P(('row', 'col')), as said below
Outputs:
- purified: bfloat16 [512, 16, 128, 128], P(('row', 'col'))
Inputs may be any that keep to these rules, and one draw needn't show every extreme that they name: `block_cols`: block row i lists 16 distinct block columns, all within cyclic distance 8 of i, in increasing order of their offset (j - i) taken in -8 .. 8; block column j is listed in row i exactly when i is listed in row j. `blocks`: the matrix is symmetric: the block listed for (i, j) is the transpose of the block listed for (j, i).
All inputs are finite; a program needn't handle non-finite values.
Results may differ from a plain program's by a relative error of at most 0.0039.
Values may be sent and summed in bfloat16 or wider, within the bound.
A program may use at most 64 MiB of HBM per device.

v0:
```python
import jax
import jax.numpy as jnp
from jax import lax
from jax.sharding import PartitionSpec as P

BAND = 8


def passed_along(value, axis, steps):
    count = lax.axis_size(axis)
    pairs = [(source, (source + steps) % count) for source in range(count)]
    return lax.ppermute(value, axis, pairs)


def neighbour(piece, distance):
    return passed_along(piece, ("row", "col"), distance)


def mirrored(piece, distance):
    return passed_along(piece, ("row", "col"), distance)


def band_apply(factor, window_rows, start_slot, stop_slot):
    window = 2 * BAND + 1
    own_rows = factor.shape[0]
    result = jnp.zeros((own_rows, window) + factor.shape[2:], jnp.float32)
    for offset in range(window):
        first_slot = max(start_slot, offset - BAND)
        last_slot = min(stop_slot, offset + BAND + 1)
        source = window_rows[
            offset : offset + own_rows, first_slot - offset + BAND : last_slot - offset + BAND
        ]
        partial_value = jnp.einsum(
            "rxy,rlyz->rlxz", factor[:, offset], source, preferred_element_type=jnp.float32
        )
        result = result.at[:, first_slot:last_slot].add(partial_value)
    return result


def per_device(block_cols, blocks):
    own_rows = blocks.shape[0]
    all_rows = own_rows * lax.axis_size(("row", "col"))
    first_row = lax.axis_index(("row", "col")) * own_rows
    row_ids = first_row + jnp.arange(own_rows, dtype=jnp.int32)
    offsets = (block_cols - row_ids[:, None] + BAND) % all_rows
    selector = offsets[:, :, None] == jnp.arange(2 * BAND + 1, dtype=jnp.int32)[None, None, :]
    onehot = selector.astype(jnp.bfloat16)
    present = jnp.sum(selector.astype(jnp.float32), axis=1)[:, :, None, None]
    banded = jnp.einsum(
        "rsb,rsxy->rbxy", onehot, blocks, preferred_element_type=jnp.float32
    ).astype(jnp.bfloat16)
    reach_devs = BAND // own_rows
    lower_list = []
    upper_list = []
    for distance in range(1, reach_devs + 1):
        lower_list.append(neighbour(banded, distance))
        upper_list.append(neighbour(banded, -distance))
    window_rows = jnp.concatenate(lower_list[::-1] + [banded] + upper_list, axis=0)
    upper_part = band_apply(banded, window_rows, BAND, 2 * BAND + 1)[:, BAND:]
    upper_blocks = (upper_part * present[:, BAND:]).astype(jnp.bfloat16)
    sent_list = []
    for distance in range(reach_devs, 0, -1):
        sent_list.append(mirrored(upper_blocks, distance))
    mirror_rows = jnp.concatenate(sent_list + [upper_blocks], axis=0)
    lower_blocks = [
        jnp.swapaxes(mirror_rows[target : target + own_rows, BAND - target], -1, -2)
        for target in range(BAND)
    ]
    squared = jnp.concatenate([jnp.stack(lower_blocks, axis=1), upper_blocks], axis=1)
    cubic = band_apply(squared, window_rows, 0, 2 * BAND + 1) * present
    newband = (3.0 * squared.astype(jnp.float32) - 2.0 * cubic).astype(jnp.bfloat16)
    return jnp.einsum("rsb,rbxy->rsxy", onehot, newband, preferred_element_type=jnp.float32).astype(
        jnp.bfloat16
    )


def solution(mesh):
    placed = (P(("row", "col"), None), P(("row", "col"), None, None, None))
    return jax.shard_map(
        per_device,
        mesh=mesh,
        in_specs=placed,
        out_specs=P(("row", "col"), None, None, None),
        check_vma=False,
    )
```

profile of v0, /device:TPU:68, one launch (start us, length us, event | category | flops | bytes accessed | tf_op | source)
XLA Modules:
  0.0 359.0 jit_solution(1542366307266053961)
XLA Ops:
  0.0 0.7 fusion.100
  1.7 4.3 %collective-permute-start = (bf16[1,17,128,128]{3,2,1,0:T(8,128)(2,1)S(1)}, bf16[1,17,128,128]{3,2,1,0:T(8,128)(2,1)S(1)}, u32[]{:S(2)}, u32[]{:S(2)}) collective-permute-start(bf16[1,17,128,128]{3,2,1,0:T(8,128)(2,1)S(1)} %copy.178), channel_id=1, source_target_pairs={{0,8},{1,9},{2,10},{3,11},{4,12},{5,13},{6,14},{7,15},{8,16},{9,17... | collective-permute-start | bytes 1671176 | tf_op jit(solution)/shard_map/ppermute | solution.py:12
  6.0 5.4 %collective-permute-start.1 = (bf16[1,17,128,128]{3,2,1,0:T(8,128)(2,1)S(1)}, bf16[1,17,128,128]{3,2,1,0:T(8,128)(2,1)S(1)}, u32[]{:S(2)}, u32[]{:S(2)}) collective-permute-start(bf16[1,17,128,128]{3,2,1,0:T(8,128)(2,1)S(1)} %copy.178), channel_id=1, source_target_pairs={{0,7},{1,8},{2,9},{3,10},{4,11},{5,12},{6,13},{7,14},{8,15},{9,16}... | collective-permute-start | bytes 1671176 | tf_op jit(solution)/shard_map/ppermute | solution.py:12
  11.4 5.9 %collective-permute-start.2 = (bf16[1,17,128,128]{3,2,1,0:T(8,128)(2,1)S(1)}, bf16[1,17,128,128]{3,2,1,0:T(8,128)(2,1)S(1)}, u32[]{:S(2)}, u32[]{:S(2)}) collective-permute-start(bf16[1,17,128,128]{3,2,1,0:T(8,128)(2,1)S(1)} %copy.178), channel_id=1, source_target_pairs={{0,6},{1,7},{2,8},{3,9},{4,10},{5,11},{6,12},{7,13},{8,14},{9,15},... | collective-permute-start | bytes 1671176 | tf_op jit(solution)/shard_map/ppermute | solution.py:12
  17.3 2.7 collective-permute-start.3
  20.0 5.7 %collective-permute-start.4 = (bf16[1,17,128,128]{3,2,1,0:T(8,128)(2,1)S(1)}, bf16[1,17,128,128]{3,2,1,0:T(8,128)(2,1)S(1)}, u32[]{:S(2)}, u32[]{:S(2)}) collective-permute-start(bf16[1,17,128,128]{3,2,1,0:T(8,128)(2,1)S(1)} %copy.178), channel_id=1, source_target_pairs={{0,4},{1,5},{2,6},{3,7},{4,8},{5,9},{6,10},{7,11},{8,12},{9,13},{1... | collective-permute-start | bytes 1671176 | tf_op jit(solution)/shard_map/ppermute | solution.py:12
  25.7 1.0 fusion.102
  26.9 34.3 %collective-permute-done = bf16[1,17,128,128]{3,2,1,0:T(8,128)(2,1)S(1)} collective-permute-done((bf16[1,17,128,128]{3,2,1,0:T(8,128)(2,1)S(1)}, bf16[1,17,128,128]{3,2,1,0:T(8,128)(2,1)S(1)}, u32[]{:S(2)}, u32[]{:S(2)}) %collective-permute-start) | collective-permute-done | bytes 557088 | tf_op jit(solution)/shard_map/ppermute | solution.py:12
  61.1 1.9 collective-permute-start.5
  63.4 1.9 collective-permute-start.14
  65.5 1.9 collective-permute-start.13
  67.7 18.3 %collective-permute-done.3 = bf16[1,17,128,128]{3,2,1,0:T(8,128)(2,1)S(1)} collective-permute-done((bf16[1,17,128,128]{3,2,1,0:T(8,128)(2,1)S(1)}, bf16[1,17,128,128]{3,2,1,0:T(8,128)(2,1)S(1)}, u32[]{:S(2)}, u32[]{:S(2)}) %collective-permute-start.3) | collective-permute-done | bytes 557088 | tf_op jit(solution)/shard_map/ppermute | solution.py:12
  86.0 1.9 collective-permute-start.12
  88.2 8.5 %collective-permute-start.11 = (bf16[1,17,128,128]{3,2,1,0:T(8,128)(2,1)S(1)}, bf16[1,17,128,128]{3,2,1,0:T(8,128)(2,1)S(1)}, u32[]{:S(2)}, u32[]{:S(2)}) collective-permute-start(bf16[1,17,128,128]{3,2,1,0:T(8,128)(2,1)S(1)} %copy.178), channel_id=1, source_target_pairs={{0,508},{1,509},{2,510},{3,511},{4,0},{5,1},{6,2},{7,3},{8,4},{9,5... | collective-permute-start | bytes 1671176 | tf_op jit(solution)/shard_map/ppermute | solution.py:12
  97.0 25.1 %collective-permute-start.10 = (bf16[1,17,128,128]{3,2,1,0:T(8,128)(2,1)S(1)}, bf16[1,17,128,128]{3,2,1,0:T(8,128)(2,1)S(1)}, u32[]{:S(2)}, u32[]{:S(2)}) collective-permute-start(bf16[1,17,128,128]{3,2,1,0:T(8,128)(2,1)S(1)} %copy.178), channel_id=1, source_target_pairs={{0,509},{1,510},{2,511},{3,0},{4,1},{5,2},{6,3},{7,4},{8,5},{9,6},... | collective-permute-start | bytes 1671176 | tf_op jit(solution)/shard_map/ppermute | solution.py:12
  122.4 19.3 %collective-permute-done.14 = bf16[1,17,128,128]{3,2,1,0:T(8,128)(2,1)S(1)} collective-permute-done((bf16[1,17,128,128]{3,2,1,0:T(8,128)(2,1)S(1)}, bf16[1,17,128,128]{3,2,1,0:T(8,128)(2,1)S(1)}, u32[]{:S(2)}, u32[]{:S(2)}) %collective-permute-start.14) | collective-permute-done | bytes 557088 | tf_op jit(solution)/shard_map/ppermute | solution.py:12
  141.7 41.7 %collective-permute-start.9 = (bf16[1,17,128,128]{3,2,1,0:T(8,128)(2,1)S(1)}, bf16[1,17,128,128]{3,2,1,0:T(8,128)(2,1)S(1)}, u32[]{:S(2)}, u32[]{:S(2)}) collective-permute-start(bf16[1,17,128,128]{3,2,1,0:T(8,128)(2,1)S(1)} %copy.178), channel_id=1, source_target_pairs={{0,510},{1,511},{2,0},{3,1},{4,2},{5,3},{6,4},{7,5},{8,6},{9,7},{1... | collective-permute-start | bytes 1671176 | tf_op jit(solution)/shard_map/ppermute | solution.py:12
  183.8 3.9 %collective-permute-start.6 = (bf16[1,17,128,128]{3,2,1,0:T(8,128)(2,1)S(1)}, bf16[1,17,128,128]{3,2,1,0:T(8,128)(2,1)S(1)}, u32[]{:S(2)}, u32[]{:S(2)}) collective-permute-start(bf16[1,17,128,128]{3,2,1,0:T(8,128)(2,1)S(1)} %copy.178), channel_id=1, source_target_pairs={{0,2},{1,3},{2,4},{3,5},{4,6},{5,7},{6,8},{7,9},{8,10},{9,11},{10,... | collective-permute-start | bytes 1671176 | tf_op jit(solution)/shard_map/ppermute | solution.py:12
  188.0 4.3 %collective-permute-start.7 = (bf16[1,17,128,128]{3,2,1,0:T(8,128)(2,1)S(1)}, bf16[1,17,128,128]{3,2,1,0:T(8,128)(2,1)S(1)}, u32[]{:S(2)}, u32[]{:S(2)}) collective-permute-start(bf16[1,17,128,128]{3,2,1,0:T(8,128)(2,1)S(1)} %copy.178), channel_id=1, source_target_pairs={{0,1},{1,2},{2,3},{3,4},{4,5},{5,6},{6,7},{7,8},{8,9},{9,10},{10,1... | collective-permute-start | bytes 1671176 | tf_op jit(solution)/shard_map/ppermute | solution.py:12
  192.6 30.9 %collective-permute-done.11 = bf16[1,17,128,128]{3,2,1,0:T(8,128)(2,1)S(1)} collective-permute-done((bf16[1,17,128,128]{3,2,1,0:T(8,128)(2,1)S(1)}, bf16[1,17,128,128]{3,2,1,0:T(8,128)(2,1)S(1)}, u32[]{:S(2)}, u32[]{:S(2)}) %collective-permute-start.11) | collective-permute-done | bytes 557088 | tf_op jit(solution)/shard_map/ppermute | solution.py:12
  223.4 1.9 collective-permute-start.15
  225.7 6.7 %collective-permute-done.10 = bf16[1,17,128,128]{3,2,1,0:T(8,128)(2,1)S(1)} collective-permute-done((bf16[1,17,128,128]{3,2,1,0:T(8,128)(2,1)S(1)}, bf16[1,17,128,128]{3,2,1,0:T(8,128)(2,1)S(1)}, u32[]{:S(2)}, u32[]{:S(2)}) %collective-permute-start.10) | collective-permute-done | bytes 557088 | tf_op jit(solution)/shard_map/ppermute | solution.py:12
  232.3 12.9 %collective-permute-start.8 = (bf16[1,17,128,128]{3,2,1,0:T(8,128)(2,1)S(1)}, bf16[1,17,128,128]{3,2,1,0:T(8,128)(2,1)S(1)}, u32[]{:S(2)}, u32[]{:S(2)}) collective-permute-start(bf16[1,17,128,128]{3,2,1,0:T(8,128)(2,1)S(1)} %copy.178), channel_id=1, source_target_pairs={{0,511},{1,0},{2,1},{3,2},{4,3},{5,4},{6,5},{7,6},{8,7},{9,8},{10,... | collective-permute-start | bytes 1671176 | tf_op jit(solution)/shard_map/ppermute | solution.py:12
  245.5 8.5 %collective-permute-done.9 = bf16[1,17,128,128]{3,2,1,0:T(8,128)(2,1)S(1)} collective-permute-done((bf16[1,17,128,128]{3,2,1,0:T(8,128)(2,1)S(1)}, bf16[1,17,128,128]{3,2,1,0:T(8,128)(2,1)S(1)}, u32[]{:S(2)}, u32[]{:S(2)}) %collective-permute-start.9) | collective-permute-done | bytes 557088 | tf_op jit(solution)/shard_map/ppermute | solution.py:12
  255.6 11.7 %collective-permute-done.8 = bf16[1,17,128,128]{3,2,1,0:T(8,128)(2,1)S(1)} collective-permute-done((bf16[1,17,128,128]{3,2,1,0:T(8,128)(2,1)S(1)}, bf16[1,17,128,128]{3,2,1,0:T(8,128)(2,1)S(1)}, u32[]{:S(2)}, u32[]{:S(2)}) %collective-permute-start.8) | collective-permute-done | bytes 557088 | tf_op jit(solution)/shard_map/ppermute | solution.py:12
  267.7 0.9 copy.210
  268.6 2.0 collective-permute-start.16
  270.7 1.9 collective-permute-start.17
  272.6 1.9 collective-permute-start.18
  274.5 1.9 collective-permute-start.19
  276.4 1.9 collective-permute-start.20
  278.4 8.1 %collective-permute-done.16 = bf16[1,9,128,128]{3,2,1,0:T(8,128)(2,1)S(1)} collective-permute-done((bf16[1,9,128,128]{3,2,1,0:T(8,128)(2,1)}, bf16[1,9,128,128]{3,2,1,0:T(8,128)(2,1)S(1)}, u32[]{:S(2)}, u32[]{:S(2)}) %collective-permute-start.16) | collective-permute-done | bytes 294944 | tf_op jit(solution)/shard_map/ppermute | solution.py:12
  286.5 5.6 %collective-permute-start.21 = (bf16[1,9,128,128]{3,2,1,0:T(8,128)(2,1)}, bf16[1,9,128,128]{3,2,1,0:T(8,128)(2,1)S(1)}, u32[]{:S(2)}, u32[]{:S(2)}) collective-permute-start(bf16[1,9,128,128]{3,2,1,0:T(8,128)(2,1)} %copy.210), channel_id=1, source_target_pairs={{0,3},{1,4},{2,5},{3,6},{4,7},{5,8},{6,9},{7,10},{8,11},{9,12},{10... | collective-permute-start | bytes 884744 | tf_op jit(solution)/shard_map/ppermute | solution.py:12
  292.1 18.8 %collective-permute-start.22 = (bf16[1,9,128,128]{3,2,1,0:T(8,128)(2,1)}, bf16[1,9,128,128]{3,2,1,0:T(8,128)(2,1)S(1)}, u32[]{:S(2)}, u32[]{:S(2)}) collective-permute-start(bf16[1,9,128,128]{3,2,1,0:T(8,128)(2,1)} %copy.210), channel_id=1, source_target_pairs={{0,2},{1,3},{2,4},{3,5},{4,6},{5,7},{6,8},{7,9},{8,10},{9,11},{10,... | collective-permute-start | bytes 884744 | tf_op jit(solution)/shard_map/ppermute | solution.py:12
  311.0 2.1 collective-permute-start.23
  313.1 11.3 %collective-permute-done.19 = bf16[1,9,128,128]{3,2,1,0:T(8,128)(2,1)S(1)} collective-permute-done((bf16[1,9,128,128]{3,2,1,0:T(8,128)(2,1)}, bf16[1,9,128,128]{3,2,1,0:T(8,128)(2,1)S(1)}, u32[]{:S(2)}, u32[]{:S(2)}) %collective-permute-start.19) | collective-permute-done | bytes 294944 | tf_op jit(solution)/shard_map/ppermute | solution.py:12
  324.6 11.0 %collective-permute-done.22 = bf16[1,9,128,128]{3,2,1,0:T(8,128)(2,1)S(1)} collective-permute-done((bf16[1,9,128,128]{3,2,1,0:T(8,128)(2,1)}, bf16[1,9,128,128]{3,2,1,0:T(8,128)(2,1)S(1)}, u32[]{:S(2)}, u32[]{:S(2)}) %collective-permute-start.22) | collective-permute-done | bytes 294944 | tf_op jit(solution)/shard_map/ppermute | solution.py:12
  335.6 6.9 %collective-permute-done.23 = bf16[1,9,128,128]{3,2,1,0:T(8,128)(2,1)S(1)} collective-permute-done((bf16[1,9,128,128]{3,2,1,0:T(8,128)(2,1)}, bf16[1,9,128,128]{3,2,1,0:T(8,128)(2,1)S(1)}, u32[]{:S(2)}, u32[]{:S(2)}) %collective-permute-start.23) | collective-permute-done | bytes 294944 | tf_op jit(solution)/shard_map/ppermute | solution.py:12
  343.9 0.8 copy-done.22
  345.0 0.7 copy-done.20
  346.1 0.7 copy-done.18
  348.2 0.7 copy-done.4
  351.8 0.7 copy-done.6
  352.9 0.7 copy-done.8
  353.9 0.7 copy-done.10
  355.0 0.8 copy-done.14
  356.0 0.8 copy-done.16
  358.1 0.9 copy.244
  (112 shorter events, 15.0 us)
Async XLA Ops:
  0.0 1.1 copy-start
  1.7 59.4 %collective-permute-start = (bf16[1,17,128,128]{3,2,1,0:T(8,128)(2,1)S(1)}, bf16[1,17,128,128]{3,2,1,0:T(8,128)(2,1)S(1)}, u32[]{:S(2)}, u32[]{:S(2)}) collective-permute-start(bf16[1,17,128,128]{3,2,1,0:T(8,128)(2,1)S(1)} %copy.178), channel_id=1, source_target_pairs={{0,8},{1,9},{2,10},{3,11},{4,12},{5,13},{6,14},{7,15},{8,16},{9,17... | collective-permute-start | bytes 1671176 | tf_op jit(solution)/shard_map/ppermute | solution.py:12
  6.0 57.3 %collective-permute-start.1 = (bf16[1,17,128,128]{3,2,1,0:T(8,128)(2,1)S(1)}, bf16[1,17,128,128]{3,2,1,0:T(8,128)(2,1)S(1)}, u32[]{:S(2)}, u32[]{:S(2)}) collective-permute-start(bf16[1,17,128,128]{3,2,1,0:T(8,128)(2,1)S(1)} %copy.178), channel_id=1, source_target_pairs={{0,7},{1,8},{2,9},{3,10},{4,11},{5,12},{6,13},{7,14},{8,15},{9,16}... | collective-permute-start | bytes 1671176 | tf_op jit(solution)/shard_map/ppermute | solution.py:12
  11.4 54.1 %collective-permute-start.2 = (bf16[1,17,128,128]{3,2,1,0:T(8,128)(2,1)S(1)}, bf16[1,17,128,128]{3,2,1,0:T(8,128)(2,1)S(1)}, u32[]{:S(2)}, u32[]{:S(2)}) collective-permute-start(bf16[1,17,128,128]{3,2,1,0:T(8,128)(2,1)S(1)} %copy.178), channel_id=1, source_target_pairs={{0,6},{1,7},{2,8},{3,9},{4,10},{5,11},{6,12},{7,13},{8,14},{9,15},... | collective-permute-start | bytes 1671176 | tf_op jit(solution)/shard_map/ppermute | solution.py:12
  17.3 68.7 %collective-permute-start.3 = (bf16[1,17,128,128]{3,2,1,0:T(8,128)(2,1)S(1)}, bf16[1,17,128,128]{3,2,1,0:T(8,128)(2,1)S(1)}, u32[]{:S(2)}, u32[]{:S(2)}) collective-permute-start(bf16[1,17,128,128]{3,2,1,0:T(8,128)(2,1)S(1)} %copy.178), channel_id=1, source_target_pairs={{0,5},{1,6},{2,7},{3,8},{4,9},{5,10},{6,11},{7,12},{8,13},{9,14},{... | collective-permute-start | bytes 1671176 | tf_op jit(solution)/shard_map/ppermute | solution.py:12
  20.0 68.2 %collective-permute-start.4 = (bf16[1,17,128,128]{3,2,1,0:T(8,128)(2,1)S(1)}, bf16[1,17,128,128]{3,2,1,0:T(8,128)(2,1)S(1)}, u32[]{:S(2)}, u32[]{:S(2)}) collective-permute-start(bf16[1,17,128,128]{3,2,1,0:T(8,128)(2,1)S(1)} %copy.178), channel_id=1, source_target_pairs={{0,4},{1,5},{2,6},{3,7},{4,8},{5,9},{6,10},{7,11},{8,12},{9,13},{1... | collective-permute-start | bytes 1671176 | tf_op jit(solution)/shard_map/ppermute | solution.py:12
  61.1 27.0 %copy-start.25 = (bf16[1,17,128,128]{3,2,1,0:T(8,128)(2,1)}, bf16[1,17,128,128]{3,2,1,0:T(8,128)(2,1)S(1)}, u32[]{:S(2)}) copy-start(bf16[1,17,128,128]{3,2,1,0:T(8,128)(2,1)S(1)} %collective-permute-done) | copy-start | bytes 1671172
  61.1 35.8 %collective-permute-start.5 = (bf16[1,17,128,128]{3,2,1,0:T(8,128)(2,1)S(1)}, bf16[1,17,128,128]{3,2,1,0:T(8,128)(2,1)S(1)}, u32[]{:S(2)}, u32[]{:S(2)}) collective-permute-start(bf16[1,17,128,128]{3,2,1,0:T(8,128)(2,1)S(1)} %copy.178), channel_id=1, source_target_pairs={{0,3},{1,4},{2,5},{3,6},{4,7},{5,8},{6,9},{7,10},{8,11},{9,12},{10... | collective-permute-start | bytes 1671176 | tf_op jit(solution)/shard_map/ppermute | solution.py:12
  63.4 33.6 %copy-start.23 = (bf16[1,17,128,128]{3,2,1,0:T(8,128)(2,1)}, bf16[1,17,128,128]{3,2,1,0:T(8,128)(2,1)S(1)}, u32[]{:S(2)}) copy-start(bf16[1,17,128,128]{3,2,1,0:T(8,128)(2,1)S(1)} %collective-permute-done.1) | copy-start | bytes 1671172
  63.4 78.3 %collective-permute-start.14 = (bf16[1,17,128,128]{3,2,1,0:T(8,128)(2,1)S(1)}, bf16[1,17,128,128]{3,2,1,0:T(8,128)(2,1)S(1)}, u32[]{:S(2)}, u32[]{:S(2)}) collective-permute-start(bf16[1,17,128,128]{3,2,1,0:T(8,128)(2,1)S(1)} %copy.178), channel_id=1, source_target_pairs={{0,505},{1,506},{2,507},{3,508},{4,509},{5,510},{6,511},{7,0},{8,1... | collective-permute-start | bytes 1671176 | tf_op jit(solution)/shard_map/ppermute | solution.py:12
  65.5 56.9 %copy-start.21 = (bf16[1,17,128,128]{3,2,1,0:T(8,128)(2,1)}, bf16[1,17,128,128]{3,2,1,0:T(8,128)(2,1)S(1)}, u32[]{:S(2)}) copy-start(bf16[1,17,128,128]{3,2,1,0:T(8,128)(2,1)S(1)} %collective-permute-done.2) | copy-start | bytes 1671172
  65.5 118.2 %collective-permute-start.13 = (bf16[1,17,128,128]{3,2,1,0:T(8,128)(2,1)S(1)}, bf16[1,17,128,128]{3,2,1,0:T(8,128)(2,1)S(1)}, u32[]{:S(2)}, u32[]{:S(2)}) collective-permute-start(bf16[1,17,128,128]{3,2,1,0:T(8,128)(2,1)S(1)} %copy.178), channel_id=1, source_target_pairs={{0,506},{1,507},{2,508},{3,509},{4,510},{5,511},{6,0},{7,1},{8,2},... | collective-permute-start | bytes 1671176 | tf_op jit(solution)/shard_map/ppermute | solution.py:12
  86.0 36.4 %copy-start.19 = (bf16[1,17,128,128]{3,2,1,0:T(8,128)(2,1)}, bf16[1,17,128,128]{3,2,1,0:T(8,128)(2,1)S(1)}, u32[]{:S(2)}) copy-start(bf16[1,17,128,128]{3,2,1,0:T(8,128)(2,1)S(1)} %collective-permute-done.3) | copy-start | bytes 1671172
  86.0 101.9 %collective-permute-start.12 = (bf16[1,17,128,128]{3,2,1,0:T(8,128)(2,1)S(1)}, bf16[1,17,128,128]{3,2,1,0:T(8,128)(2,1)S(1)}, u32[]{:S(2)}, u32[]{:S(2)}) collective-permute-start(bf16[1,17,128,128]{3,2,1,0:T(8,128)(2,1)S(1)} %copy.178), channel_id=1, source_target_pairs={{0,507},{1,508},{2,509},{3,510},{4,511},{5,0},{6,1},{7,2},{8,3},{9... | collective-permute-start | bytes 1671176 | tf_op jit(solution)/shard_map/ppermute | solution.py:12
  88.2 95.6 %copy-start.17 = (bf16[1,17,128,128]{3,2,1,0:T(8,128)(2,1)}, bf16[1,17,128,128]{3,2,1,0:T(8,128)(2,1)S(1)}, u32[]{:S(2)}) copy-start(bf16[1,17,128,128]{3,2,1,0:T(8,128)(2,1)S(1)} %collective-permute-done.4) | copy-start | bytes 1671172
  88.2 135.2 %collective-permute-start.11 = (bf16[1,17,128,128]{3,2,1,0:T(8,128)(2,1)S(1)}, bf16[1,17,128,128]{3,2,1,0:T(8,128)(2,1)S(1)}, u32[]{:S(2)}, u32[]{:S(2)}) collective-permute-start(bf16[1,17,128,128]{3,2,1,0:T(8,128)(2,1)S(1)} %copy.178), channel_id=1, source_target_pairs={{0,508},{1,509},{2,510},{3,511},{4,0},{5,1},{6,2},{7,3},{8,4},{9,5... | collective-permute-start | bytes 1671176 | tf_op jit(solution)/shard_map/ppermute | solution.py:12
  97.0 90.9 %copy-start.11 = (bf16[1,17,128,128]{3,2,1,0:T(8,128)(2,1)}, bf16[1,17,128,128]{3,2,1,0:T(8,128)(2,1)S(1)}, u32[]{:S(2)}) copy-start(bf16[1,17,128,128]{3,2,1,0:T(8,128)(2,1)S(1)} %collective-permute-done.5) | copy-start | bytes 1671172
  97.0 135.3 %collective-permute-start.10 = (bf16[1,17,128,128]{3,2,1,0:T(8,128)(2,1)S(1)}, bf16[1,17,128,128]{3,2,1,0:T(8,128)(2,1)S(1)}, u32[]{:S(2)}, u32[]{:S(2)}) collective-permute-start(bf16[1,17,128,128]{3,2,1,0:T(8,128)(2,1)S(1)} %copy.178), channel_id=1, source_target_pairs={{0,509},{1,510},{2,511},{3,0},{4,1},{5,2},{6,3},{7,4},{8,5},{9,6},... | collective-permute-start | bytes 1671176 | tf_op jit(solution)/shard_map/ppermute | solution.py:12
  141.7 42.0 %copy-start.13 = (bf16[1,17,128,128]{3,2,1,0:T(8,128)(2,1)}, bf16[1,17,128,128]{3,2,1,0:T(8,128)(2,1)S(1)}, u32[]{:S(2)}) copy-start(bf16[1,17,128,128]{3,2,1,0:T(8,128)(2,1)S(1)} %collective-permute-done.14) | copy-start | bytes 1671172
  141.7 112.2 %collective-permute-start.9 = (bf16[1,17,128,128]{3,2,1,0:T(8,128)(2,1)S(1)}, bf16[1,17,128,128]{3,2,1,0:T(8,128)(2,1)S(1)}, u32[]{:S(2)}, u32[]{:S(2)}) collective-permute-start(bf16[1,17,128,128]{3,2,1,0:T(8,128)(2,1)S(1)} %copy.178), channel_id=1, source_target_pairs={{0,510},{1,511},{2,0},{3,1},{4,2},{5,3},{6,4},{7,5},{8,6},{9,7},{1... | collective-permute-start | bytes 1671176 | tf_op jit(solution)/shard_map/ppermute | solution.py:12
  183.8 41.9 %copy-start.9 = (bf16[1,17,128,128]{3,2,1,0:T(8,128)(2,1)}, bf16[1,17,128,128]{3,2,1,0:T(8,128)(2,1)S(1)}, u32[]{:S(2)}) copy-start(bf16[1,17,128,128]{3,2,1,0:T(8,128)(2,1)S(1)} %collective-permute-done.13) | copy-start | bytes 1671172
  183.8 70.4 %collective-permute-start.6 = (bf16[1,17,128,128]{3,2,1,0:T(8,128)(2,1)S(1)}, bf16[1,17,128,128]{3,2,1,0:T(8,128)(2,1)S(1)}, u32[]{:S(2)}, u32[]{:S(2)}) collective-permute-start(bf16[1,17,128,128]{3,2,1,0:T(8,128)(2,1)S(1)} %copy.178), channel_id=1, source_target_pairs={{0,2},{1,3},{2,4},{3,5},{4,6},{5,7},{6,8},{7,9},{8,10},{9,11},{10,... | collective-permute-start | bytes 1671176 | tf_op jit(solution)/shard_map/ppermute | solution.py:12
  187.9 57.5 %copy-start.7 = (bf16[1,17,128,128]{3,2,1,0:T(8,128)(2,1)}, bf16[1,17,128,128]{3,2,1,0:T(8,128)(2,1)S(1)}, u32[]{:S(2)}) copy-start(bf16[1,17,128,128]{3,2,1,0:T(8,128)(2,1)S(1)} %collective-permute-done.12) | copy-start | bytes 1671172
  188.0 66.9 %collective-permute-start.7 = (bf16[1,17,128,128]{3,2,1,0:T(8,128)(2,1)S(1)}, bf16[1,17,128,128]{3,2,1,0:T(8,128)(2,1)S(1)}, u32[]{:S(2)}, u32[]{:S(2)}) collective-permute-start(bf16[1,17,128,128]{3,2,1,0:T(8,128)(2,1)S(1)} %copy.178), channel_id=1, source_target_pairs={{0,1},{1,2},{2,3},{3,4},{4,5},{5,6},{6,7},{7,8},{8,9},{9,10},{10,1... | collective-permute-start | bytes 1671176 | tf_op jit(solution)/shard_map/ppermute | solution.py:12
  223.4 2.2 copy-start.5
  223.4 31.1 %collective-permute-start.15 = (bf16[1,17,128,128]{3,2,1,0:T(8,128)(2,1)S(1)}, bf16[1,17,128,128]{3,2,1,0:T(8,128)(2,1)S(1)}, u32[]{:S(2)}, u32[]{:S(2)}) collective-permute-start(bf16[1,17,128,128]{3,2,1,0:T(8,128)(2,1)S(1)} %copy.178), channel_id=1, source_target_pairs={{0,504},{1,505},{2,506},{3,507},{4,508},{5,509},{6,510},{7,511},{8... | collective-permute-start | bytes 1671176 | tf_op jit(solution)/shard_map/ppermute | solution.py:12
  232.3 22.2 %copy-start.1 = (bf16[1,17,128,128]{3,2,1,0:T(8,128)(2,1)}, bf16[1,17,128,128]{3,2,1,0:T(8,128)(2,1)S(1)}, u32[]{:S(2)}) copy-start(bf16[1,17,128,128]{3,2,1,0:T(8,128)(2,1)S(1)} %collective-permute-done.10) | copy-start | bytes 1671172
  232.3 35.0 %collective-permute-start.8 = (bf16[1,17,128,128]{3,2,1,0:T(8,128)(2,1)S(1)}, bf16[1,17,128,128]{3,2,1,0:T(8,128)(2,1)S(1)}, u32[]{:S(2)}, u32[]{:S(2)}) collective-permute-start(bf16[1,17,128,128]{3,2,1,0:T(8,128)(2,1)S(1)} %copy.178), channel_id=1, source_target_pairs={{0,511},{1,0},{2,1},{3,2},{4,3},{5,4},{6,5},{7,6},{8,7},{9,8},{10,... | collective-permute-start | bytes 1671176 | tf_op jit(solution)/shard_map/ppermute | solution.py:12
  268.6 74.0 %copy-start.26 = (bf16[1,17,128,128]{3,2,1,0:T(8,128)(2,1)S(1)}, bf16[1,17,128,128]{3,2,1,0:T(8,128)(2,1)}, u32[]{:S(2)}) copy-start(bf16[1,17,128,128]{3,2,1,0:T(8,128)(2,1)} %copy-done.25) | copy-start | bytes 1671172
  268.6 17.9 %collective-permute-start.16 = (bf16[1,9,128,128]{3,2,1,0:T(8,128)(2,1)}, bf16[1,9,128,128]{3,2,1,0:T(8,128)(2,1)S(1)}, u32[]{:S(2)}, u32[]{:S(2)}) collective-permute-start(bf16[1,9,128,128]{3,2,1,0:T(8,128)(2,1)} %copy.210), channel_id=1, source_target_pairs={{0,8},{1,9},{2,10},{3,11},{4,12},{5,13},{6,14},{7,15},{8,16},{9,17... | collective-permute-start | bytes 884744 | tf_op jit(solution)/shard_map/ppermute | solution.py:12
  270.7 21.4 %collective-permute-start.17 = (bf16[1,9,128,128]{3,2,1,0:T(8,128)(2,1)}, bf16[1,9,128,128]{3,2,1,0:T(8,128)(2,1)S(1)}, u32[]{:S(2)}, u32[]{:S(2)}) collective-permute-start(bf16[1,9,128,128]{3,2,1,0:T(8,128)(2,1)} %copy.210), channel_id=1, source_target_pairs={{0,7},{1,8},{2,9},{3,10},{4,11},{5,12},{6,13},{7,14},{8,15},{9,16}... | collective-permute-start | bytes 884744 | tf_op jit(solution)/shard_map/ppermute | solution.py:12
  272.6 38.4 %collective-permute-start.18 = (bf16[1,9,128,128]{3,2,1,0:T(8,128)(2,1)}, bf16[1,9,128,128]{3,2,1,0:T(8,128)(2,1)S(1)}, u32[]{:S(2)}, u32[]{:S(2)}) collective-permute-start(bf16[1,9,128,128]{3,2,1,0:T(8,128)(2,1)} %copy.210), channel_id=1, source_target_pairs={{0,6},{1,7},{2,8},{3,9},{4,10},{5,11},{6,12},{7,13},{8,14},{9,15},... | collective-permute-start | bytes 884744 | tf_op jit(solution)/shard_map/ppermute | solution.py:12
  274.5 49.8 %collective-permute-start.19 = (bf16[1,9,128,128]{3,2,1,0:T(8,128)(2,1)}, bf16[1,9,128,128]{3,2,1,0:T(8,128)(2,1)S(1)}, u32[]{:S(2)}, u32[]{:S(2)}) collective-permute-start(bf16[1,9,128,128]{3,2,1,0:T(8,128)(2,1)} %copy.210), channel_id=1, source_target_pairs={{0,5},{1,6},{2,7},{3,8},{4,9},{5,10},{6,11},{7,12},{8,13},{9,14},{... | collective-permute-start | bytes 884744 | tf_op jit(solution)/shard_map/ppermute | solution.py:12
  276.4 47.9 %collective-permute-start.20 = (bf16[1,9,128,128]{3,2,1,0:T(8,128)(2,1)}, bf16[1,9,128,128]{3,2,1,0:T(8,128)(2,1)S(1)}, u32[]{:S(2)}, u32[]{:S(2)}) collective-permute-start(bf16[1,9,128,128]{3,2,1,0:T(8,128)(2,1)} %copy.210), channel_id=1, source_target_pairs={{0,4},{1,5},{2,6},{3,7},{4,8},{5,9},{6,10},{7,11},{8,12},{9,13},{1... | collective-permute-start | bytes 884744 | tf_op jit(solution)/shard_map/ppermute | solution.py:12
  286.5 38.1 %collective-permute-start.21 = (bf16[1,9,128,128]{3,2,1,0:T(8,128)(2,1)}, bf16[1,9,128,128]{3,2,1,0:T(8,128)(2,1)S(1)}, u32[]{:S(2)}, u32[]{:S(2)}) collective-permute-start(bf16[1,9,128,128]{3,2,1,0:T(8,128)(2,1)} %copy.210), channel_id=1, source_target_pairs={{0,3},{1,4},{2,5},{3,6},{4,7},{5,8},{6,9},{7,10},{8,11},{9,12},{10... | collective-permute-start | bytes 884744 | tf_op jit(solution)/shard_map/ppermute | solution.py:12
  292.1 43.5 %collective-permute-start.22 = (bf16[1,9,128,128]{3,2,1,0:T(8,128)(2,1)}, bf16[1,9,128,128]{3,2,1,0:T(8,128)(2,1)S(1)}, u32[]{:S(2)}, u32[]{:S(2)}) collective-permute-start(bf16[1,9,128,128]{3,2,1,0:T(8,128)(2,1)} %copy.210), channel_id=1, source_target_pairs={{0,2},{1,3},{2,4},{3,5},{4,6},{5,7},{6,8},{7,9},{8,10},{9,11},{10,... | collective-permute-start | bytes 884744 | tf_op jit(solution)/shard_map/ppermute | solution.py:12
  311.0 31.5 %collective-permute-start.23 = (bf16[1,9,128,128]{3,2,1,0:T(8,128)(2,1)}, bf16[1,9,128,128]{3,2,1,0:T(8,128)(2,1)S(1)}, u32[]{:S(2)}, u32[]{:S(2)}) collective-permute-start(bf16[1,9,128,128]{3,2,1,0:T(8,128)(2,1)} %copy.210), channel_id=1, source_target_pairs={{0,1},{1,2},{2,3},{3,4},{4,5},{5,6},{6,7},{7,8},{8,9},{9,10},{10,1... | collective-permute-start | bytes 884744 | tf_op jit(solution)/shard_map/ppermute | solution.py:12
  342.6 1.1 copy-start.24
  343.6 1.1 copy-start.22
  344.7 1.1 copy-start.20
  345.7 1.1 copy-start.18
  346.8 1.1 copy-start.12
  347.8 1.1 copy-start.4
  350.4 1.1 copy-start.2
  351.5 1.1 copy-start.6
  352.6 1.1 copy-start.8
  353.6 1.1 copy-start.10
  354.7 1.1 copy-start.14
  (3 other events, 2.7 us)
where the time goes:
time: 360 us; the launch traced here: 359 us
  waiting for transfers between devices  167 us (46%)
  starting transfers between devices  166 us (46%)
  local copies, waits for them, and re-layouts  13.2 us (4%)
  matrix products  10.7 us (3%)
    ppermute x24, waiting for transfers between devices, passed_along(): return lax.ppermute(value, axis, pairs)  167 us
    ppermute x24, starting transfers between devices, passed_along(): return lax.ppermute(value, axis, pairs)  166 us
    dot_general x34, matrix products, band_apply(): jnp.einsum('rxy,rlyz->rlxz', factor[:, offset], source, preferred_element...  9.82 us
    unnamed x62, local copies, waits for them, and re-layouts  9.45 us
  transfers between devices with their start and end apart: 24, of which 12 were waited for; matrix products, arithmetic and copies ran while one was open for 1% of the time, Pallas kernels for 0%

commit v1 on v0

v1 whole, which is shorter than its diff:
```python
import functools

import jax
import jax.numpy as jnp
from jax import lax
from jax.experimental import pallas as pl
from jax.experimental.pallas import tpu as pltpu
from jax.sharding import PartitionSpec as P

BAND = 8
WINDOW = 2 * BAND + 1
HALF = BAND + 1
RING = 8
MESH = pl.DeviceIdType.MESH

EVENTS = (
    (1, 16200, 231488, 86344, 12088, 231488, 7976, 223264, 219152),
    (1, 131144, 16200, 16200, 86344, 16200, 231488, 86344, 24352),
    (1, 68426, 131144, 131401, 131658, 131144, 86601, 17485, 86344),
    (1, 221208, 86858, 221208, 221208, 86601, 131915, 132429, 131144),
    (1, 67912, 14144, 86858, 14144, 10032, 16200, 86601, 71952),
    (1, 17485, 86601, 17999, 86601, 86858, 69896, 18256, 28464),
    (1, 131401, 131915, 229432, 227376, 225320, 227376, 227376, 221208),
    (1, 223264, 221208, 132172, 131144, 132172, 131144, 132686, 132943),
    (1, 68169, 17485, 12088, 16200, 12088, 12088, 86858, 30520),
    (1, 17742, 69896, 74008, 87115, 69896, 86344, 17742, 86601),
    (1, 68940, 17999, 14144, 87372, 17485, 86858, 17999, 32576),
    (1, 18256, 71952, 87115, 17742, 71952, 17228, 69896, 86858),
    (1, 131658, 233544, 231488, 229432, 131401, 223264, 231488, 223264),
    (1, 225320, 131401, 131144, 131401, 223264, 131401, 131144, 131915),
    (1, 69197, 18256, 233544, 18256, 17999, 225320, 233544, 87115),
    (1, 10032, 223264, 18256, 231488, 131658, 71952, 131401, 132172),
    (0, 83, 63, 63, 63, 47, 63, 31, 11),
    (1, 233544, 74008, 69896, 131915, 18256, 13887, 87115, 18184),
    (0, 95, 81, 81, 82, 82, 81, 81, 68),
    (1, 69968, 10032, 13887, 88914, 88914, 88657, 88657, 69896),
    (0, 0, 0, 1, 2, 0, 3, 5, 0),
    (0, 96, 136, 96, 96, 136, 136, 104, 88),
    (1, 12088, 133457, 133457, 13887, 227119, 32648, 24424, 217867),
    (1, 137055, 67840, 68097, 69896, 67840, 87629, 71952, 16128),
    (1, 70739, 13887, 17228, 132429, 32648, 131658, 223007, 74008),
    (0, 82, 68, 55, 70, 17, 39, 25, 9),
    (0, 111, 83, 82, 83, 55, 82, 63, 71),
    (1, 14144, 225320, 71952, 219152, 131915, 133714, 131658, 225320),
    (1, 219152, 133971, 219152, 89171, 72209, 7719, 13887, 132429),
    (1, 68683, 17228, 133714, 15686, 78120, 74008, 74265, 22296),
    (0, 17, 33, 68, 17, 63, 47, 47, 10),
    (0, 119, 69, 84, 47, 81, 83, 82, 69),
    (0, 1, 3, 4, 0, 4, 0, 6, 7),
    (0, 104, 96, 128, 120, 112, 120, 120, 96),
    (1, 26223, 76321, 76064, 10032, 11831, 227119, 28536, 76064),
    (1, 143223, 68611, 7976, 71952, 231231, 28536, 229432, 17927),
    (1, 131915, 227376, 134228, 132686, 227376, 229432, 9775, 132686),
    (1, 227376, 7976, 223264, 74008, 132429, 132172, 88914, 78120),
    (0, 25, 71, 70, 25, 69, 17, 67, 13),
    (0, 127, 84, 85, 55, 83, 68, 83, 70),
    (1, 74080, 134228, 11831, 68354, 13887, 68611, 133971, 34889),
    (0, 2, 1, 0, 1, 1, 1, 0, 3),
    (0, 112, 144, 136, 128, 104, 104, 136, 104),
    (1, 24424, 12088, 68868, 17485, 15429, 17742, 32648, 218381),
    (0, 9, 10, 71, 54, 71, 70, 54, 14),
    (1, 70482, 70410, 15172, 228918, 74008, 17999, 89171, 87372),
    (0, 63, 39, 91, 91, 90, 90, 84, 95),
    (1, 30335, 131658, 134485, 11574, 90970, 89171, 228918, 218638),
    (1, 132172, 229432, 15686, 132943, 229432, 233544, 131915, 160068),
    (0, 33, 17, 39, 9, 25, 71, 17, 17),
    (1, 219409, 16971, 225063, 17999, 132686, 132429, 89428, 16899),
    (0, 71, 47, 92, 71, 54, 84, 127, 54),
    (0, 23, 9, 9, 3, 2, 10, 1, 4),
    (0, 144, 104, 144, 136, 119, 112, 144, 83),
    (1, 13887, 70153, 70153, 72209, 88657, 18256, 34704, 87629),
    (1, 78192, 231231, 131658, 217353, 15943, 72209, 225320, 30006),
    (1, 132429, 17742, 225320, 133714, 233544, 132686, 132172, 228918),
    (1, 217353, 72209, 91227, 9775, 132943, 219152, 30335, 153927),
    (0, 42, 25, 17, 26, 61, 25, 30, 20),
    (0, 70, 55, 54, 67, 86, 127, 33, 111),
    (0, 47, 11, 10, 5, 3, 2, 2, 5),
    (1, 69454, 70667, 15943, 74265, 11574, 90970, 72209, 70153),
    (0, 88, 112, 88, 88, 135, 119, 103, 112),
    (1, 17999, 74265, 70410, 11831, 68868, 15172, 24167, 17156),
    (1, 86416, 5920, 11574, 91227, 89171, 70410, 74008, 70410),
    (0, 12, 41, 25, 31, 33, 34, 41, 12),
    (0, 87, 102, 67, 49, 39, 46, 111, 127),
    (1, 7976, 138854, 91484, 223007, 13373, 15686, 222750, 17413),
    (1, 132686, 132172, 131915, 133971, 133714, 221208, 133457, 137055),
    (1, 225834, 217610, 227376, 223264, 219152, 15943, 87372, 227376),
    (0, 19, 13, 31, 46, 12, 54, 49, 33),
    (0, 136, 95, 33, 99, 45, 91, 69, 38),
    (0, 3, 12, 12, 6, 5, 4, 11, 6),
    (0, 120, 120, 104, 126, 120, 128, 128, 85),
    (1, 72024, 15172, 16971, 70153, 74265, 87372, 30592, 72209),
    (1, 22368, 132429, 78120, 15943, 9261, 136027, 221208, 25894),
    (1, 132943, 218381, 231231, 136027, 133457, 231231, 26223, 141167),
    (1, 219923, 15429, 132429, 225320, 221208, 132943, 69125, 229432),
    (0, 18, 18, 11, 33, 68, 60, 70, 19),
    (0, 117, 118, 47, 59, 92, 92, 85, 135),
    (0, 4, 2, 13, 7, 6, 5, 3, 86),
    (0, 89, 128, 111, 81, 128, 144, 126, 113),
    (1, 80248, 78377, 17742, 74522, 87115, 30335, 30078, 89171),
    (1, 15943, 72466, 72209, 5920, 16971, 89428, 16971, 17670),
    (1, 3607, 71181, 74265, 93283, 28279, 28279, 69382, 72980),
    (0, 20, 19, 26, 61, 26, 62, 71, 49),
    (0, 66, 54, 66, 90, 70, 93, 86, 94),
    (1, 72281, 15943, 10032, 7976, 87629, 74265, 134742, 15217),
    (1, 133971, 219666, 228918, 231231, 133971, 225063, 133714, 145279),
    (1, 219666, 72723, 132686, 138083, 7719, 133457, 76321, 231488),
    (1, 15686, 7719, 22368, 80433, 76064, 76578, 17228, 70924),
    (0, 26, 70, 34, 13, 38, 26, 18, 15),
    (0, 67, 100, 69, 62, 99, 45, 59, 118),
    (0, 5, 30, 2, 10, 7, 6, 4, 89),
    (0, 81, 135, 112, 103, 144, 88, 112, 126),
    (1, 70225, 138340, 76321, 22368, 224806, 9518, 134228, 15961),
    (1, 133714, 219923, 136027, 229175, 229175, 226862, 219152, 147335),
    (1, 220180, 70924, 223007, 135770, 135770, 133971, 78377, 233544),
    (1, 9775, 9775, 14915, 14915, 15172, 11574, 14915, 76321),
    (0, 34, 31, 23, 45, 19, 33, 19, 81),
    (0, 68, 101, 100, 92, 46, 52, 61, 119),
    (0, 6, 4, 3, 11, 10, 19, 9, 23),
    (0, 114, 82, 120, 104, 88, 96, 102, 120),
    (1, 78706, 138597, 70924, 76321, 89942, 91227, 219923, 22039),
    (1, 27765, 76064, 70667, 9518, 15686, 13116, 80433, 89685),
    (0, 27, 49, 18, 34, 62, 36, 26, 25),
    (1, 221979, 11831, 5663, 90970, 76321, 91484, 15429, 218124),
    (0, 101, 87, 59, 66, 85, 85, 62, 117),
    (1, 145279, 132686, 217867, 226862, 228918, 228918, 145279, 136798),
    (1, 16714, 228918, 136284, 136284, 134742, 135770, 15686, 72723),
    (0, 50, 26, 35, 69, 23, 14, 92, 57),
    (0, 69, 62, 60, 84, 93, 66, 118, 102),
    (0, 7, 5, 5, 19, 9, 7, 14, 39),
    (0, 91, 85, 135, 112, 96, 135, 96, 128),
    (1, 72795, 23910, 71181, 30078, 9518, 13630, 89685, 26151),
    (1, 134999, 78120, 9775, 71181, 70924, 91741, 141167, 224806),
    (1, 229432, 132943, 138340, 134228, 225063, 226605, 227119, 169000),
    (1, 16971, 223007, 227119, 218381, 136284, 134228, 72466, 89942),
    (1, 65856, 22111, 74522, 12859, 13630, 9261, 15943, 26408),
    (0, 22, 14, 62, 39, 31, 15, 29, 26),
    (0, 59, 34, 108, 86, 34, 110, 110, 66),
    (0, 11, 28, 6, 27, 11, 9, 10, 55),
    (0, 90, 90, 126, 135, 110, 111, 91, 136),
    (1, 72538, 80176, 26223, 91484, 91484, 74522, 222493, 30263),
    (1, 32648, 75550, 16714, 13373, 7976, 76064, 72723, 80433),
    (1, 218124, 28022, 76578, 76578, 74522, 11060, 12859, 219923),
    (0, 28, 42, 30, 41, 43, 30, 21, 18),
    (0, 62, 61, 58, 87, 87, 42, 37, 67),
    (1, 142709, 218638, 140396, 226605, 138083, 145279, 220437, 131658),
    (1, 28536, 137055, 220951, 134742, 218124, 218638, 134485, 87886),
    (0, 21, 21, 38, 58, 58, 50, 42, 51),
    (0, 86, 38, 42, 95, 100, 59, 45, 58),
    (0, 10, 29, 19, 18, 18, 11, 12, 63),
    (0, 92, 91, 103, 127, 127, 118, 88, 144),
    (1, 73052, 11574, 17485, 80176, 93283, 6948, 26480, 32319),
    (1, 138597, 80433, 93540, 13630, 17742, 82232, 74522, 218895),
    (1, 221722, 220437, 222750, 134999, 226862, 218895, 136284, 158021),
    (1, 76136, 142966, 1037, 225063, 134485, 136541, 224549, 34632),
    (1, 14658, 1808, 72466, 9261, 26480, 16714, 91484, 69382),
    (0, 41, 20, 46, 22, 37, 58, 51, 28),
    (0, 102, 108, 99, 42, 101, 61, 94, 60),
    (0, 55, 6, 20, 20, 14, 18, 55, 22),
    (0, 99, 126, 83, 118, 126, 126, 101, 84),
    (1, 74851, 74522, 138083, 82232, 72723, 88914, 13373, 21782),
    (1, 14915, 3864, 14658, 16971, 102535, 76321, 23910, 100222),
    (1, 134742, 76578, 76835, 76064, 24424, 17485, 80176, 219666),
    (0, 49, 22, 22, 21, 102, 37, 28, 27),
    (0, 118, 65, 93, 38, 117, 94, 53, 61),
    (1, 223778, 224806, 136541, 220694, 136541, 222750, 226605, 155974),
    (1, 15172, 134999, 224806, 137055, 220951, 134485, 142966, 88657),
    (0, 57, 35, 86, 101, 35, 27, 36, 1),
    (0, 103, 66, 101, 102, 50, 53, 95, 62),
    (0, 15, 7, 28, 12, 20, 12, 39, 110),
    (0, 128, 103, 119, 85, 111, 117, 119, 148),
    (1, 82304, 32648, 15429, 5663, 12602, 1808, 82232, 8084),
    (1, 138854, 75036, 95596, 78120, 76578, 72723, 13630, 222236),
    (1, 227890, 220180, 138597, 220437, 134999, 224549, 222236, 142966),
    (1, 15429, 140396, 226862, 138597, 223007, 140910, 140910, 74265),
    (0, 39, 43, 43, 35, 41, 28, 43, 29),
    (0, 126, 127, 109, 65, 52, 31, 58, 50),
    (0, 45, 23, 36, 14, 27, 55, 13, 2),
    (0, 84, 86, 95, 117, 84, 86, 93, 91),
    (1, 70996, 22368, 12859, 88657, 96110, 78634, 28022, 16642),
    (1, 12859, 78634, 88143, 24167, 27765, 14658, 70667, 82489),
    (1, 220694, 15686, 82746, 14658, 78891, 80690, 21083, 221979),
    (1, 142966, 75293, 13116, 78377, 10546, 12859, 71438, 143223),
    (0, 58, 109, 45, 68, 53, 35, 27, 36),
    (0, 85, 111, 57, 108, 65, 69, 87, 103),
    (1, 13630, 220694, 134742, 138854, 224549, 221979, 136798, 74522),
    (0, 35, 27, 7, 4, 36, 101, 15, 41),
    (0, 135, 57, 65, 28, 91, 103, 65, 52),
    (0, 29, 46, 27, 15, 13, 21, 20, 87),
    (0, 98, 93, 102, 111, 118, 87, 109, 105),
    (1, 74594, 140653, 220694, 224806, 138597, 136798, 224292, 15465),
    (1, 222236, 76835, 13630, 15429, 11060, 82746, 78634, 222493),
    (1, 145022, 13630, 78634, 78634, 93540, 13373, 10803, 142709),
    (1, 30592, 221979, 140653, 222236, 224292, 222236, 137055, 80947),
    (0, 31, 44, 15, 57, 42, 57, 68, 65),
    (0, 43, 58, 41, 144, 66, 95, 135, 93),
    (0, 14, 15, 21, 23, 21, 13, 46, 90),
    (0, 106, 110, 110, 94, 95, 102, 117, 97),
    (1, 76650, 78891, 226605, 140396, 138854, 138597, 221979, 15713),
    (1, 134485, 13373, 78891, 12602, 11317, 76835, 23653, 138854),
    (1, 220437, 74779, 9518, 76835, 76835, 11317, 82746, 224292),
    (0, 37, 59, 49, 43, 22, 49, 7, 21),
    (0, 65, 117, 127, 60, 28, 65, 90, 53),
    (0, 51, 60, 87, 50, 51, 20, 34, 109),
    (0, 30, 88, 90, 119, 94, 108, 57, 46),
    (0, 122, 36, 29, 29, 15, 38, 38, 100),
    (1, 80762, 142709, 262144, 262144, 262144, 262144, 11317, 27950),
    (0, 60, 92, 118, 93, 103, 109, 100, 35),
    (0, 38, 50, 50, 51, 57, 23, 50, 82),
    (0, 46, 67, 61, 52, 59, 41, 66, 47),
    (0, 94, 37, 14, 30, 29, 22, 22, 99),
    (1, 73566, 79148, 262144, 262144, 262144, 262144, 8747, 28207),
    (0, 61, 94, 94, 110, 109, 99, 108, 43),
    (0, 44, 51, 51, 53, 60, 43, 35, 42),
    (0, 52, 53, 53, 109, 67, 51, 52, 92),
    (0, 54, 52, 44, 37, 44, 44, 44, 45),
    (0, 100, 119, 52, 44, 49, 67, 60, 101),
    (1, 75108, 262144, 262144, 262144, 262144, 262144, 262144, 27693),
    (0, 109, 45, 37, 36, 30, 29, 23, 59),
    (0, 36, 99, 117, 100, 108, 100, 99, 44),
    (0, 13, 262144, 262144, 262144, 262144, 262144, 262144, 30),
    (0, 93, 262144, 262144, 262144, 262144, 262144, 262144, 108),
    (0, 110, 262144, 262144, 262144, 262144, 262144, 262144, 31),
    (0, 53, 262144, 262144, 262144, 262144, 262144, 262144, 34),
    (0, 108, 262144, 262144, 262144, 262144, 262144, 262144, 37),
)
NONE = 2**18
OWN = BAND * HALF


def device_of(row, cols):
    return row // cols, lax.rem(row, cols)


def kernel(cols_ref, blocks_ref, out_ref, own, square, upper, flipped, newband, send_sem, recv_sem):
    size = blocks_ref.shape[-1]
    cols = lax.axis_size("col")
    count = cols * lax.axis_size("row")
    me = lax.axis_index("row") * cols + lax.axis_index("col")
    place = lax.rem(me, RING)
    start = me - place
    targets = (
        start + lax.rem(place + 1, RING),
        start + lax.rem(place + RING - 1, RING),
        lax.rem(me + RING, count),
        lax.rem(me + count - RING, count),
    )
    barrier = pltpu.get_barrier_semaphore()
    peers = [device_of(target, cols) for target in targets]
    for peer in peers:
        pl.semaphore_signal(barrier, inc=1, device_id=peer, device_id_type=MESH)

    bits = [lax.rem(place // 2**n, 2) == 1 for n in range(3)]

    def pick(values):
        for bit in bits:
            values = [jnp.where(bit, high, low) for low, high in zip(values[::2], values[1::2])]
        return values[0]

    missing = jnp.int32(0)
    for s in range(WINDOW - 1):
        offset = lax.rem(cols_ref[0, s] - me + BAND + count, count)
        missing += jnp.where(offset == s, 1, 0)

    for o in range(WINDOW):
        first = blocks_ref[0, min(o, WINDOW - 2)]
        second = blocks_ref[0, max(o - 1, 0)]
        block = jnp.where(o < missing, first, jnp.where(o == missing, jnp.zeros_like(first), second))
        own[:, o * size : (o + 1) * size] = block
        turned = block.T
        if o >= BAND:
            upper[OWN + o - BAND] = block
            flipped[OWN + o - BAND] = turned
        else:
            slot = o * HALF + BAND - o
            upper[slot] = turned
            flipped[slot] = block

    pl.semaphore_wait(barrier, len(targets))

    def copy(n, here, there, peer):
        return pltpu.make_async_remote_copy(
            src_ref=upper.at[here],
            dst_ref=upper.at[there],
            send_sem=send_sem.at[n],
            recv_sem=recv_sem.at[there],
            device_id=peer,
            device_id_type=MESH,
        )

    def send(n, code):
        direction = code >> 16
        ahead, far = (direction & 1) == 0, direction >= 2
        peer = tuple(
            jnp.where(far, jnp.where(ahead, c, d), jnp.where(ahead, a, b)) for a, b, c, d in zip(*peers)
        )
        copy(n, code & 255, (code >> 8) & 255, peer).start()

    def receive(here):
        copy(0, here, here, peers[0]).wait_recv()
        flipped[here] = upper[here].T

    def where_any(codes, code, action):
        if NONE in codes:
            pl.when(code != NONE)(action)
        else:
            action()

    sent = []
    for sends, *codes in EVENTS:
        code = pick([jnp.int32(c) for c in codes])
        if sends:
            where_any(codes, code, functools.partial(send, len(sent), code))
            sent.append((codes, code))
        else:
            where_any(codes, code, functools.partial(receive, code))

    def block_at(k, j):
        if abs(k - j) > BAND:
            return jnp.zeros((size, size), upper.dtype)
        return upper[k * HALF + j - k] if k <= j else flipped[j * HALF + k - j]

    def product(factor, first, width):
        low, high = max(0, first - BAND), min(WINDOW, first + width + BAND)
        columns = [
            jnp.concatenate([block_at(k, j) for k in range(low, high)], axis=0) for j in range(first, first + width)
        ]
        return jnp.dot(
            factor[:, low * size : high * size],
            jnp.concatenate(columns, axis=1),
            preferred_element_type=jnp.float32,
        )

    for first in range(0, WINDOW, 2):
        width = min(2, WINDOW - first)
        total = product(own, first, width)
        for w in range(width):
            piece = total[:, w * size : (w + 1) * size]
            piece = jnp.where(missing == first + w, 0.0, piece).astype(square.dtype)
            square[:, (first + w) * size : (first + w + 1) * size] = piece
    for first in range(0, WINDOW, 2):
        width = min(2, WINDOW - first)
        total = product(square, first, width)
        for w in range(width):
            part = slice((first + w) * size, (first + w + 1) * size)
            value = 3.0 * square[:, part].astype(jnp.float32) - 2.0 * total[:, w * size : (w + 1) * size]
            newband[first + w] = value.astype(newband.dtype)
    for s in range(WINDOW - 1):
        out_ref[0, s] = jnp.where(s < missing, newband[s], newband[s + 1])

    for n, (codes, code) in enumerate(sent):
        where_any(codes, code, lambda n=n: copy(n, OWN, OWN, peers[0]).wait_send())


def per_device(block_cols, blocks):
    size = blocks.shape[-1]
    kind = blocks.dtype
    sends = sum(event[0] for event in EVENTS)
    return pl.pallas_call(
        kernel,
        out_shape=jax.ShapeDtypeStruct(blocks.shape, kind),
        in_specs=[pl.BlockSpec(memory_space=pltpu.SMEM), pl.BlockSpec(memory_space=pltpu.VMEM)],
        out_specs=pl.BlockSpec(memory_space=pltpu.VMEM),
        scratch_shapes=[
            pltpu.VMEM((size, WINDOW * size), kind),
            pltpu.VMEM((size, WINDOW * size), kind),
            pltpu.VMEM((WINDOW * HALF, size, size), kind),
            pltpu.VMEM((WINDOW * HALF, size, size), kind),
            pltpu.VMEM((WINDOW, size, size), kind),
            pltpu.SemaphoreType.DMA((sends,)),
            pltpu.SemaphoreType.DMA((WINDOW * HALF,)),
        ],
        compiler_params=pltpu.CompilerParams(collective_id=0, has_side_effects=True, vmem_limit_bytes=40 * 2**20),
        cost_estimate=pl.CostEstimate(flops=4 * 217 * size**3, bytes_accessed=2 * 2**20, transcendentals=0),
        name="purify",
    )(block_cols, blocks)


def solution(mesh):
    placed = (P(("row", "col"), None), P(("row", "col"), None, None, None))
    return jax.shard_map(
        per_device,
        mesh=mesh,
        in_specs=placed,
        out_specs=P(("row", "col"), None, None, None),
        check_vma=False,
    )
```

time: 360 us -> 52.2 us (0.15)
  the two profiles are of different devices: /device:TPU:68 before, /device:TPU:6 now
where the time goes in v1:
time: 52.2 us; the launch traced here: 52.1 us
  Pallas kernels  49.6 us (95%)
  local copies, waits for them, and re-layouts  2.49 us (5%)
    pallas_call x1, Pallas kernels, per_device(): pl.pallas_call(kernel, out_shape=jax.ShapeDtypeStruct(blocks.shape, kind)...  49.6 us
    unnamed x5, local copies, waits for them, and re-layouts  2.49 us

profile of v1, /device:TPU:6, one launch (start us, length us, event | category | flops | bytes accessed | tf_op | source)
XLA Modules:
  0.0 52.1 jit_solution(4306061201126987992)
XLA Ops:
  0.0 0.0 copy-start
  0.0 1.0 %copy-done = bf16[1,16,128,128]{3,2,1,0:T(8,128)(2,1)S(1)} copy-done((bf16[1,16,128,128]{3,2,1,0:T(8,128)(2,1)S(1)}, bf16[1,16,128,128]{3,2,1,0:T(8,128)(2,1)}, u32[]{:S(2)}) %copy-start) | copy-done | bytes 524312
  1.0 0.0 copy-start.1
  1.0 0.7 %copy-done.1 = s32[1,16]{1,0:T(1,128)S(1)} copy-done((s32[1,16]{1,0:T(1,128)S(1)}, s32[1,16]{1,0:T(1,128)}, u32[]{:S(2)}) %copy-start.1) | copy-done | bytes 88
  1.7 49.6 %purify.1 = bf16[1,16,128,128]{3,2,1,0:T(8,128)(2,1)S(1)} custom-call(s32[1,16]{1,0:T(1,128)S(1)} %copy-done.1, bf16[1,16,128,128]{3,2,1,0:T(8,128)(2,1)S(1)} %copy-done), custom_call_target="tpu_custom_call" | custom-call | flops 1820327936 | bytes 2097152 | tf_op jit(solution)/shard_map/purify/pallas_call | solution.py:358
  51.3 0.8 %copy.4 = bf16[1,16,128,128]{3,2,1,0:T(8,128)(2,1)} copy(bf16[1,16,128,128]{3,2,1,0:T(8,128)(2,1)S(1)} %purify.1) | data formatting | bytes 1048576
Async XLA Ops:
  0.0 1.0 %copy-start = (bf16[1,16,128,128]{3,2,1,0:T(8,128)(2,1)S(1)}, bf16[1,16,128,128]{3,2,1,0:T(8,128)(2,1)}, u32[]{:S(2)}) copy-start(bf16[1,16,128,128]{3,2,1,0:T(8,128)(2,1)} %blocks_ref.1) | copy-start | bytes 1572868
  1.0 0.7 %copy-start.1 = (s32[1,16]{1,0:T(1,128)S(1)}, s32[1,16]{1,0:T(1,128)}, u32[]{:S(2)}) copy-start(s32[1,16]{1,0:T(1,128)} %cols_ref.1) | copy-start | bytes 196

commit v2 on v0

v2 whole, which is shorter than its diff:
```python
import functools

import jax
import jax.numpy as jnp
from jax import lax
from jax.experimental import pallas as pl
from jax.experimental.pallas import tpu as pltpu
from jax.sharding import PartitionSpec as P

BAND = 8
WINDOW = 2 * BAND + 1
HALF = BAND + 1
RING = 8
MESH = pl.DeviceIdType.MESH

EVENTS = (
    (1, 16200, 231488, 229432, 231488, 225320, 223264, 221208, 223264),
    (1, 67912, 14144, 14144, 14144, 7976, 86344, 12088, 34632),
    (1, 131144, 86344, 86344, 86344, 86344, 16200, 86344, 86344),
    (1, 219152, 132429, 131915, 131401, 131144, 131915, 131144, 132943),
    (1, 68169, 16200, 16200, 16200, 14144, 14144, 14144, 32576),
    (1, 14144, 86601, 86601, 86601, 86601, 86601, 86601, 86601),
    (1, 233544, 233544, 231488, 227376, 227376, 229432, 223264, 169248),
    (1, 131401, 131144, 132172, 132429, 131401, 131144, 131401, 225320),
    (1, 68426, 86858, 86858, 86858, 16200, 86858, 16200, 26408),
    (1, 17742, 18256, 18256, 17742, 69896, 17228, 69896, 69896),
    (1, 233801, 131401, 12088, 229432, 10032, 225320, 225320, 71952),
    (1, 131658, 17999, 233544, 131144, 229432, 131401, 86858, 227376),
    (1, 17999, 69896, 132429, 87115, 86858, 17999, 131658, 28464),
    (1, 69968, 219152, 69896, 17999, 131658, 69896, 22792, 132429),
    (1, 131915, 71952, 17742, 18256, 12088, 18256, 87115, 74008),
    (1, 221208, 131658, 74008, 233544, 87115, 71952, 229432, 30520),
    (1, 68683, 221208, 131401, 131658, 231488, 131658, 131915, 229432),
    (1, 18256, 10032, 219152, 10032, 131915, 10032, 10032, 132686),
    (1, 223264, 87115, 17999, 69896, 17485, 233544, 71952, 86858),
    (1, 10032, 223264, 76064, 12088, 71952, 87115, 231488, 18184),
    (1, 12088, 12088, 221208, 131915, 233544, 132172, 17228, 169744),
    (1, 17228, 87372, 10032, 219152, 17999, 74008, 132172, 231488),
    (1, 132172, 131915, 131144, 71952, 74008, 132429, 17742, 87115),
    (0, 81, 63, 55, 55, 55, 31, 63, 9),
    (1, 70225, 225320, 223264, 74008, 18256, 227376, 233544, 168504),
    (0, 135, 81, 81, 81, 81, 81, 81, 47),
    (1, 32391, 80176, 131658, 132172, 132172, 132686, 132429, 233544),
    (1, 68940, 17485, 225320, 221208, 219152, 223007, 17999, 168256),
    (1, 17485, 227376, 88657, 76064, 132429, 88657, 74008, 28207),
    (0, 0, 5, 3, 1, 0, 3, 0, 7),
    (0, 88, 136, 128, 136, 112, 104, 96, 104),
    (1, 72024, 13887, 133457, 132686, 221208, 76064, 132686, 70153),
    (1, 132429, 88657, 11831, 223264, 88657, 17742, 13887, 17927),
    (1, 235343, 17742, 68611, 88657, 11831, 24424, 88657, 131144),
    (0, 82, 55, 63, 63, 63, 55, 55, 10),
    (1, 70482, 132172, 132686, 11831, 132686, 231488, 76064, 70410),
    (0, 127, 82, 82, 82, 82, 82, 82, 55),
    (1, 30335, 229432, 227376, 17485, 88914, 132943, 227376, 30263),
    (0, 1, 0, 4, 5, 1, 0, 1, 11),
    (1, 3864, 11831, 13887, 132943, 13887, 11831, 132943, 70667),
    (0, 83, 69, 71, 17, 69, 17, 17, 63),
    (0, 103, 83, 83, 71, 83, 63, 67, 112),
    (1, 139111, 88914, 88914, 225320, 133971, 88914, 88914, 32319),
    (1, 70739, 3864, 17228, 13887, 89171, 78120, 11831, 22296),
    (0, 144, 144, 136, 120, 120, 128, 104, 149),
    (1, 86416, 133971, 68868, 88914, 15429, 231231, 87372, 76064),
    (1, 5920, 89171, 15943, 87372, 132943, 30592, 72209, 131658),
    (0, 17, 17, 70, 47, 17, 39, 25, 17),
    (1, 225320, 231231, 89171, 5920, 223264, 13887, 14915, 72209),
    (0, 111, 70, 84, 83, 70, 83, 70, 89),
    (1, 141167, 132686, 229175, 15943, 72209, 72209, 133457, 15961),
    (1, 219409, 5920, 17485, 72209, 15686, 133457, 87629, 6037),
    (1, 7976, 72209, 133971, 229175, 87372, 87372, 15686, 78120),
    (0, 2, 1, 5, 0, 2, 1, 2, 5),
    (0, 145, 88, 144, 128, 128, 112, 112, 120),
    (1, 86673, 7976, 71952, 133457, 17228, 221208, 22368, 131915),
    (0, 25, 33, 54, 69, 25, 47, 33, 18),
    (1, 227376, 132943, 89428, 78120, 231231, 7719, 87886, 219666),
    (0, 119, 126, 90, 84, 71, 84, 71, 54),
    (1, 221465, 229175, 5920, 7976, 133457, 87629, 133714, 228918),
    (1, 28279, 30078, 231231, 32648, 74265, 26480, 223521, 72466),
    (0, 3, 2, 1, 2, 3, 2, 3, 6),
    (0, 71, 41, 17, 25, 39, 25, 39, 12),
    (0, 90, 71, 39, 70, 90, 68, 83, 39),
    (1, 72538, 145022, 134228, 89171, 15943, 133714, 15943, 30006),
    (0, 96, 96, 88, 144, 136, 103, 128, 128),
    (1, 74080, 76321, 11574, 231231, 87629, 9775, 74265, 87372),
    (1, 132686, 15429, 90970, 133714, 17742, 87886, 24424, 17413),
    (1, 229432, 78377, 69125, 9775, 90970, 24167, 76321, 218124),
    (1, 15943, 15686, 7976, 89428, 225063, 229175, 26480, 225063),
    (0, 84, 39, 25, 33, 47, 70, 84, 25),
    (1, 70996, 69125, 228918, 227119, 133714, 15172, 133971, 26151),
    (0, 110, 90, 47, 39, 84, 90, 95, 67),
    (1, 25966, 90970, 135770, 133971, 76064, 89171, 7719, 132172),
    (0, 31, 11, 9, 3, 11, 4, 4, 136),
    (0, 104, 104, 96, 88, 144, 144, 136, 151),
    (1, 76136, 225063, 15686, 15429, 5920, 133971, 89171, 87629),
    (1, 135770, 15943, 72209, 74265, 227119, 15686, 137055, 87886),
    (0, 70, 12, 33, 46, 33, 71, 18, 19),
    (0, 85, 47, 46, 90, 46, 91, 46, 69),
    (1, 71253, 70924, 74265, 15686, 7719, 89428, 219152, 17670),
    (1, 15686, 218124, 7719, 76321, 89428, 225063, 226862, 162115),
    (0, 39, 3, 0, 4, 4, 5, 5, 20),
    (0, 57, 91, 41, 54, 54, 26, 19, 70),
    (0, 89, 112, 104, 91, 88, 46, 119, 144),
    (0, 118, 118, 117, 96, 91, 135, 144, 146),
    (1, 142966, 7719, 225063, 134228, 135770, 134228, 22111, 219923),
    (1, 229689, 91227, 76321, 225063, 226862, 15943, 89428, 70924),
    (1, 72281, 133457, 9775, 90970, 9518, 74265, 72466, 1943),
    (1, 134228, 227119, 78377, 7719, 76321, 9518, 28279, 220180),
    (0, 91, 13, 68, 62, 26, 33, 20, 27),
    (0, 126, 67, 91, 92, 62, 54, 54, 46),
    (1, 145022, 9775, 9518, 226862, 228918, 227119, 229175, 74265),
    (1, 72795, 71181, 227119, 9518, 11574, 90970, 134228, 158021),
    (1, 16971, 28022, 136027, 135770, 91227, 135770, 220180, 221979),
    (0, 4, 54, 2, 6, 5, 6, 6, 90),
    (0, 97, 120, 112, 104, 96, 120, 105, 145),
    (1, 74337, 74008, 91227, 91227, 136027, 228918, 72723, 27950),
    (1, 140910, 218381, 27765, 11574, 13630, 91227, 11574, 72723),
    (0, 62, 68, 26, 26, 41, 41, 26, 13),
    (1, 230974, 136027, 226862, 91484, 74522, 136027, 225063, 12178),
    (0, 92, 92, 69, 45, 68, 60, 69, 58),
    (1, 73052, 136284, 16714, 228918, 78120, 13116, 143223, 226862),
    (1, 24167, 16714, 74522, 136027, 16714, 74522, 72980, 155974),
    (0, 5, 4, 6, 7, 6, 7, 7, 0),
    (0, 26, 15, 15, 34, 23, 61, 27, 61),
    (0, 117, 99, 85, 67, 49, 85, 30, 81),
    (1, 27765, 76064, 134485, 13630, 220951, 13373, 17485, 72980),
    (1, 221722, 138083, 82232, 74522, 80176, 80176, 221979, 14225),
    (0, 151, 128, 120, 112, 119, 136, 120, 126),
    (1, 134485, 67840, 16971, 226605, 16971, 134485, 222750, 218381),
    (0, 42, 23, 23, 68, 31, 62, 41, 62),
    (0, 87, 25, 49, 99, 85, 86, 103, 82),
    (1, 26223, 16971, 218895, 9261, 134485, 13630, 30592, 80176),
    (1, 225834, 142966, 3864, 76578, 223007, 16971, 74522, 16128),
    (1, 5663, 218895, 78120, 138083, 9775, 68611, 139111, 164410),
    (1, 65856, 68097, 220951, 16714, 87886, 134742, 78120, 82232),
    (0, 46, 6, 11, 9, 7, 9, 9, 2),
    (0, 112, 135, 127, 127, 104, 96, 118, 84),
    (0, 23, 31, 31, 23, 86, 67, 38, 33),
    (0, 50, 93, 92, 85, 127, 87, 49, 87),
    (1, 136027, 17228, 136284, 93283, 134742, 76321, 32648, 16642),
    (1, 227890, 220951, 15172, 134485, 70667, 17485, 224806, 158269),
    (1, 88215, 136541, 80176, 220951, 15172, 78377, 80176, 74779),
    (0, 54, 7, 12, 10, 9, 10, 10, 3),
    (0, 68, 14, 60, 31, 38, 34, 85, 21),
    (0, 99, 110, 93, 86, 87, 69, 92, 95),
    (1, 7719, 68354, 136541, 80176, 224806, 34704, 34704, 220437),
    (0, 120, 127, 135, 135, 135, 126, 94, 99),
    (1, 74851, 1808, 15429, 16971, 134999, 134999, 136798, 16899),
    (0, 14, 26, 34, 41, 60, 23, 59, 41),
    (1, 142709, 14915, 68097, 17228, 78377, 220951, 24681, 88657),
    (1, 28022, 70667, 223007, 87629, 28279, 32391, 88143, 156222),
    (0, 102, 62, 61, 61, 92, 42, 86, 103),
    (1, 78192, 140910, 70153, 134742, 136284, 89685, 134485, 88914),
    (0, 6, 20, 18, 11, 10, 11, 11, 4),
    (0, 128, 111, 126, 119, 111, 127, 99, 111),
    (0, 21, 34, 42, 30, 61, 30, 61, 22),
    (1, 231488, 223007, 5663, 223007, 80433, 222750, 74779, 17156),
    (0, 69, 101, 62, 93, 93, 92, 87, 30),
    (1, 30078, 91484, 13116, 14915, 5663, 136284, 15429, 134999),
    (1, 80248, 11574, 80433, 68097, 136541, 76578, 134742, 220694),
    (0, 18, 27, 19, 12, 18, 12, 21, 26),
    (0, 100, 42, 30, 38, 30, 37, 23, 86),
    (0, 109, 61, 99, 42, 34, 93, 62, 91),
    (1, 134999, 218638, 138083, 136541, 30335, 11574, 78377, 222750),
    (1, 220951, 138597, 222750, 222750, 89685, 224549, 28022, 76321),
    (0, 129, 84, 111, 111, 118, 111, 88, 121),
    (1, 82304, 15172, 13373, 15172, 222750, 78634, 220437, 14969),
    (1, 13630, 74265, 76578, 69125, 13116, 14915, 21340, 137055),
    (0, 7, 50, 38, 37, 37, 27, 34, 28),
    (0, 22, 108, 100, 100, 99, 45, 37, 110),
    (1, 218638, 74522, 138340, 89685, 91484, 136541, 80433, 93283),
    (1, 138083, 5663, 224806, 5663, 224549, 221979, 134999, 222236),
    (1, 75108, 140396, 13630, 224806, 138083, 226605, 224549, 78377),
    (0, 12, 9, 13, 18, 19, 18, 12, 92),
    (0, 134, 119, 119, 118, 126, 119, 127, 105),
    (1, 9518, 72980, 78634, 138340, 13373, 30078, 12859, 15465),
    (0, 33, 66, 101, 35, 45, 28, 28, 34),
    (1, 11574, 13630, 138597, 13373, 76578, 91484, 89685, 139111),
    (0, 47, 100, 109, 108, 100, 53, 51, 45),
    (1, 82561, 138340, 140653, 78377, 226605, 222236, 222236, 27693),
    (1, 220437, 76578, 7462, 224549, 138340, 15429, 93283, 226605),
    (0, 38, 19, 20, 19, 13, 19, 29, 29),
    (0, 41, 35, 35, 49, 35, 29, 47, 68),
    (0, 55, 85, 65, 65, 53, 65, 52, 97),
    (1, 138854, 13373, 76835, 140396, 11317, 222493, 13373, 74522),
    (0, 98, 94, 118, 126, 95, 95, 111, 118),
    (0, 9, 65, 43, 57, 36, 35, 53, 36),
    (1, 83846, 74779, 78891, 7462, 76835, 11317, 222493, 15713),
    (0, 63, 102, 66, 66, 57, 66, 57, 119),
    (0, 13, 46, 21, 27, 14, 13, 31, 85),
    (0, 114, 87, 87, 117, 103, 102, 102, 130),
    (0, 10, 22, 67, 15, 12, 38, 65, 1),
    (0, 65, 49, 108, 87, 65, 49, 66, 127),
    (1, 15172, 78634, 140396, 78634, 224292, 76835, 76578, 134742),
    (1, 220694, 80690, 262144, 76835, 262144, 262144, 13630, 222493),
    (1, 138340, 76835, 262144, 262144, 262144, 262144, 10803, 76578),
    (1, 74594, 262144, 262144, 262144, 262144, 262144, 11060, 12674),
    (1, 15429, 262144, 262144, 262144, 262144, 262144, 11317, 224292),
    (1, 78706, 262144, 262144, 262144, 262144, 262144, 262144, 140910),
    (0, 11, 21, 7, 13, 15, 14, 22, 88),
    (0, 19, 30, 27, 20, 42, 57, 36, 93),
    (0, 66, 57, 57, 59, 66, 59, 68, 106),
    (1, 140653, 262144, 262144, 262144, 262144, 262144, 262144, 13418),
    (0, 122, 95, 95, 95, 110, 109, 110, 135),
    (0, 20, 10, 58, 50, 50, 88, 90, 49),
    (0, 67, 109, 86, 60, 67, 110, 135, 96),
    (0, 45, 38, 28, 14, 20, 15, 13, 94),
    (0, 136, 103, 103, 103, 102, 99, 93, 98),
    (1, 80762, 262144, 262144, 262144, 262144, 262144, 262144, 13666),
    (0, 58, 18, 10, 22, 58, 22, 91, 57),
    (0, 101, 117, 45, 58, 94, 36, 126, 60),
    (0, 15, 29, 14, 21, 21, 20, 14, 15),
    (0, 34, 53, 29, 51, 43, 50, 42, 65),
    (0, 60, 58, 59, 94, 59, 117, 45, 102),
    (0, 95, 86, 102, 102, 109, 118, 109, 109),
    (0, 35, 37, 22, 52, 22, 51, 58, 37),
    (0, 108, 43, 94, 101, 51, 58, 108, 83),
    (0, 27, 36, 37, 28, 27, 21, 15, 23),
    (0, 86, 45, 110, 110, 117, 100, 100, 100),
    (0, 29, 51, 50, 43, 52, 52, 50, 50),
    (0, 61, 28, 53, 53, 101, 94, 117, 66),
    (0, 30, 44, 36, 29, 28, 44, 35, 31),
    (0, 43, 59, 51, 36, 29, 101, 60, 52),
    (0, 49, 52, 52, 44, 44, 108, 101, 71),
    (0, 93, 60, 44, 109, 108, 43, 43, 117),
    (0, 36, 262144, 262144, 262144, 262144, 262144, 44, 35),
    (0, 52, 262144, 262144, 262144, 262144, 262144, 262144, 53),
    (0, 28, 262144, 262144, 262144, 262144, 262144, 262144, 14),
    (0, 94, 262144, 262144, 262144, 262144, 262144, 262144, 101),
    (0, 51, 262144, 262144, 262144, 262144, 262144, 262144, 42),
    (0, 53, 262144, 262144, 262144, 262144, 262144, 262144, 51),
    (0, 37, 262144, 262144, 262144, 262144, 262144, 262144, 38),
    (0, 59, 262144, 262144, 262144, 262144, 262144, 262144, 43),
    (0, 44, 262144, 262144, 262144, 262144, 262144, 262144, 59),
    (0, 262144, 262144, 262144, 262144, 262144, 262144, 262144, 108),
    (0, 262144, 262144, 262144, 262144, 262144, 262144, 262144, 44),
)
NONE = 2**18
OWN = BAND * HALF


def device_of(row, cols):
    return row // cols, lax.rem(row, cols)


def kernel(cols_hbm, blocks_hbm, out_ref, cols_ref, blocks_ref, own, square, upper, flipped, newband, in_sem, send_sem, recv_sem):
    size = blocks_ref.shape[-1]
    loads = [
        pltpu.make_async_copy(cols_hbm, cols_ref, in_sem.at[0]),
        pltpu.make_async_copy(blocks_hbm, blocks_ref, in_sem.at[1]),
    ]
    for load in loads:
        load.start()
    cols = lax.axis_size("col")
    count = cols * lax.axis_size("row")
    me = lax.axis_index("row") * cols + lax.axis_index("col")
    place = lax.rem(me, RING)
    start = me - place
    targets = (
        start + lax.rem(place + 1, RING),
        start + lax.rem(place + RING - 1, RING),
        lax.rem(me + RING, count),
        lax.rem(me + count - RING, count),
    )
    barrier = pltpu.get_barrier_semaphore()
    peers = [device_of(target, cols) for target in targets]
    for peer in peers:
        pl.semaphore_signal(barrier, inc=1, device_id=peer, device_id_type=MESH)

    bits = [lax.rem(place // 2**n, 2) == 1 for n in range(3)]

    def pick(values):
        for bit in bits:
            values = [jnp.where(bit, high, low) for low, high in zip(values[::2], values[1::2])]
        return values[0]

    for load in loads:
        load.wait()
    missing = jnp.int32(0)
    for s in range(WINDOW - 1):
        offset = lax.rem(cols_ref[0, s] - me + BAND + count, count)
        missing += jnp.where(offset == s, 1, 0)

    for o in range(WINDOW):
        first = blocks_ref[0, min(o, WINDOW - 2)]
        second = blocks_ref[0, max(o - 1, 0)]
        block = jnp.where(o < missing, first, jnp.where(o == missing, jnp.zeros_like(first), second))
        own[:, o * size : (o + 1) * size] = block
        turned = block.T
        if o >= BAND:
            upper[OWN + o - BAND] = block
            flipped[OWN + o - BAND] = turned
        else:
            slot = o * HALF + BAND - o
            upper[slot] = turned
            flipped[slot] = block

    pl.semaphore_wait(barrier, len(targets))

    def copy(n, here, there, peer):
        return pltpu.make_async_remote_copy(
            src_ref=upper.at[here],
            dst_ref=upper.at[there],
            send_sem=send_sem.at[n],
            recv_sem=recv_sem.at[there],
            device_id=peer,
            device_id_type=MESH,
        )

    def send(n, code):
        direction = code >> 16
        ahead, far = (direction & 1) == 0, direction >= 2
        peer = tuple(
            jnp.where(far, jnp.where(ahead, c, d), jnp.where(ahead, a, b)) for a, b, c, d in zip(*peers)
        )
        copy(n, code & 255, (code >> 8) & 255, peer).start()

    def receive(here):
        copy(0, here, here, peers[0]).wait_recv()
        flipped[here] = upper[here].T

    def where_any(codes, code, action):
        if NONE in codes:
            pl.when(code != NONE)(action)
        else:
            action()

    sent = []
    for sends, *codes in EVENTS:
        code = pick([jnp.int32(c) for c in codes])
        if sends:
            where_any(codes, code, functools.partial(send, len(sent), code))
            sent.append((codes, code))
        else:
            where_any(codes, code, functools.partial(receive, code))

    def block_at(k, j):
        if abs(k - j) > BAND:
            return jnp.zeros((size, size), upper.dtype)
        return upper[k * HALF + j - k] if k <= j else flipped[j * HALF + k - j]

    def product(factor, first, width):
        low, high = max(0, first - BAND), min(WINDOW, first + width + BAND)
        columns = [
            jnp.concatenate([block_at(k, j) for k in range(low, high)], axis=0) for j in range(first, first + width)
        ]
        return jnp.dot(
            factor[:, low * size : high * size],
            jnp.concatenate(columns, axis=1),
            preferred_element_type=jnp.float32,
        )

    for first in range(0, WINDOW, 2):
        width = min(2, WINDOW - first)
        total = product(own, first, width)
        for w in range(width):
            piece = total[:, w * size : (w + 1) * size]
            piece = jnp.where(missing == first + w, 0.0, piece).astype(square.dtype)
            square[:, (first + w) * size : (first + w + 1) * size] = piece
    for first in range(0, WINDOW, 2):
        width = min(2, WINDOW - first)
        total = product(square, first, width)
        for w in range(width):
            part = slice((first + w) * size, (first + w + 1) * size)
            value = 3.0 * square[:, part].astype(jnp.float32) - 2.0 * total[:, w * size : (w + 1) * size]
            newband[first + w] = value.astype(newband.dtype)
    for s in range(WINDOW - 1):
        out_ref[0, s] = jnp.where(s < missing, newband[s], newband[s + 1])

    for n, (codes, code) in enumerate(sent):
        where_any(codes, code, lambda n=n: copy(n, OWN, OWN, peers[0]).wait_send())


def per_device(block_cols, blocks):
    size = blocks.shape[-1]
    kind = blocks.dtype
    sends = sum(event[0] for event in EVENTS)
    return pl.pallas_call(
        kernel,
        out_shape=jax.ShapeDtypeStruct(blocks.shape, kind),
        in_specs=[pl.BlockSpec(memory_space=pltpu.HBM)] * 2,
        out_specs=pl.BlockSpec(memory_space=pltpu.VMEM),
        scratch_shapes=[
            pltpu.SMEM(block_cols.shape, block_cols.dtype),
            pltpu.VMEM(blocks.shape, kind),
            pltpu.VMEM((size, WINDOW * size), kind),
            pltpu.VMEM((size, WINDOW * size), kind),
            pltpu.VMEM((WINDOW * HALF, size, size), kind),
            pltpu.VMEM((WINDOW * HALF, size, size), kind),
            pltpu.VMEM((WINDOW, size, size), kind),
            pltpu.SemaphoreType.DMA((2,)),
            pltpu.SemaphoreType.DMA((sends,)),
            pltpu.SemaphoreType.DMA((WINDOW * HALF,)),
        ],
        compiler_params=pltpu.CompilerParams(collective_id=0, has_side_effects=True, vmem_limit_bytes=40 * 2**20),
        cost_estimate=pl.CostEstimate(flops=4 * 217 * size**3, bytes_accessed=2 * 2**20, transcendentals=0),
        name="purify",
    )(*(pltpu.with_memory_space_constraint(x, pltpu.HBM) for x in (block_cols, blocks)))


def solution(mesh):
    placed = (P(("row", "col"), None), P(("row", "col"), None, None, None))
    return jax.shard_map(
        per_device,
        mesh=mesh,
        in_specs=placed,
        out_specs=P(("row", "col"), None, None, None),
        check_vma=False,
    )
```

time: 360 us -> 41.2 us (0.11)
  the two profiles are of different devices: /device:TPU:68 before, /device:TPU:6 now
where the time goes in v2:
time: 41.2 us; the launch traced here: 41.1 us
  Pallas kernels  40.3 us (98%)
  local copies, waits for them, and re-layouts  0.8 us (2%)
    pallas_call x1, Pallas kernels, per_device(): pl.pallas_call(kernel, out_shape=jax.ShapeDtypeStruct(blocks.shape, kind)...  40.3 us

profile of v2, /device:TPU:6, one launch (start us, length us, event | category | flops | bytes accessed | tf_op | source)
XLA Modules:
  0.0 41.1 jit_solution(2471287937925968639)
XLA Ops:
  0.0 40.3 %purify.1 = bf16[1,16,128,128]{3,2,1,0:T(8,128)(2,1)S(1)} custom-call(s32[1,16]{1,0:T(1,128)} %cols_hbm.1, bf16[1,16,128,128]{3,2,1,0:T(8,128)(2,1)} %blocks_hbm.1), custom_call_target="tpu_custom_call" | custom-call | flops 1820327936 | bytes 2097152 | tf_op jit(solution)/shard_map/purify/pallas_call | solution.py:376
  40.3 0.8 %copy.4 = bf16[1,16,128,128]{3,2,1,0:T(8,128)(2,1)} copy(bf16[1,16,128,128]{3,2,1,0:T(8,128)(2,1)S(1)} %purify.1) | data formatting | bytes 1048576

commit v3 on v0

v3 whole, which is shorter than its diff:
```python
import functools

import jax
import jax.numpy as jnp
from jax import lax
from jax.experimental import pallas as pl
from jax.experimental.pallas import tpu as pltpu
from jax.sharding import PartitionSpec as P

BAND = 8
WINDOW = 2 * BAND + 1
HALF = BAND + 1
RING = 8
MESH = pl.DeviceIdType.MESH

NONE = 2**18
EVENTS = (
    (
        (1, 16200, 14144, 14144, 86344, 86344, 86344, 86344, 168504),
        (1, 67912, 86344, 86344, 16200, 16200, 16200, 16200, 32576),
        (1, 131144, 132429, 131915, 131658, 131144, 131144, 131144, 86344),
        (1, 69968, 16200, 16200, 14144, 12088, 14144, 12088, 34632),
        (1, 12088, 86601, 86601, 86601, 86601, 86601, 86601, 86601),
        (1, 131401, 131401, 131144, 131144, 131401, 131401, 131401, 169000),
        (1, 68169, 86858, 86858, 86858, 10032, 86858, 14144, 18184),
        (1, 14144, 18256, 17999, 18256, 86858, 18256, 71952, 69896),
        (1, 131658, 131658, 131401, 10032, 131658, 10032, 10032, 26408),
        (1, 68683, 69896, 87372, 131401, 87115, 131658, 131658, 168752),
        (1, 17999, 12088, 18256, 87115, 17999, 69896, 69896, 86858),
        (1, 68940, 87115, 12088, 12088, 18256, 12088, 86858, 28464),
        (1, 18256, 17999, 69896, 87372, 69896, 71952, 17999, 87115),
        (2,),
        (1, 233801, 231488, 229432, 223264, 231488, 225320, 223264, 219152),
        (1, 131915, 132172, 131658, 131915, 131915, 131915, 131915, 168256),
        (1, 234058, 233544, 17742, 17742, 132172, 231488, 221208, 87372),
        (1, 132172, 131144, 231488, 227376, 71952, 132172, 87115, 221208),
        (1, 7976, 10032, 132172, 132172, 225320, 17485, 132172, 131144),
        (1, 219152, 71952, 10032, 17999, 132429, 74008, 87372, 87629),
        (1, 132429, 219152, 132429, 229432, 7976, 132429, 227376, 87886),
        (1, 68426, 74008, 71952, 132429, 74008, 17742, 132429, 223264),
        (1, 10032, NONE, NONE, NONE, NONE, NONE, 7976, 169744),
        (1, NONE, NONE, NONE, NONE, NONE, NONE, 87629, 71952),
        (0, 81, 63, 55, 55, 63, 63, 63, 9),
        (0, 127, 81, 81, 81, 81, 81, 81, 63),
        (1, 70225, 13887, 88657, 88657, 13887, 13887, 13887, 32319),
        (1, 30335, 88657, 11831, 11831, 88657, 88657, 88657, 225320),
        (1, 233544, 221208, 233544, 231488, 227376, 231231, 229432, 74008),
        (1, 17228, 16971, 133457, 132686, 14144, 223264, 87886, 169496),
        (1, 69197, 76064, 74008, 69896, 132686, 87115, 132686, 30520),
        (1, 132686, NONE, NONE, NONE, NONE, 132686, 22792, NONE),
        (1, NONE, NONE, NONE, NONE, NONE, 17999, NONE, NONE),
        (0, 82, 47, 63, 63, 55, 47, 55, 17),
        (0, 135, 82, 82, 82, 82, 82, 82, 47),
        (1, 70482, 88914, 88914, 88914, 229175, 9775, 11831, 28207),
        (1, 32391, 9775, 13887, 13887, 11831, 88914, 88914, 70153),
        (1, 221208, 223264, 87629, 233544, 88914, 227376, 231231, 169248),
        (1, NONE, 131915, 219152, NONE, 229432, 132943, 132943, NONE),
        (1, NONE, NONE, NONE, NONE, 132943, NONE, NONE, NONE),
        (0, 71, 55, 71, 70, 71, 25, 17, 10),
        (0, 83, 83, 83, 83, 83, 39, 71, 55),
        (1, 70739, 133971, 89171, 89171, 15943, 74265, 15943, 30263),
        (1, 17485, 11831, 15943, 15686, 89171, 7719, 74008, 72209),
        (1, NONE, NONE, NONE, 17485, 17228, 87372, NONE, NONE),
        (1, NONE, NONE, NONE, 71952, NONE, NONE, NONE, NONE),
        (0, 17, 70, 47, 71, 17, 17, 39, 12),
        (0, 103, 85, 84, 84, 39, 70, 83, 39),
        (1, 223264, 134485, 227119, 89428, 133457, 229432, 225063, 26151),
        (1, 133457, 225320, 9775, 15943, 17485, 133457, 133457, 227376),
        (1, NONE, 17485, 89428, 221208, 76064, 15686, 72209, 131658),
        (1, NONE, 78120, 221208, 132943, NONE, 87629, NONE, NONE),
        (1, NONE, NONE, 17485, 74008, NONE, NONE, NONE, NONE),
        (1, NONE, NONE, 133714, 7976, NONE, NONE, NONE, NONE),
        (0, 84, 17, 70, 17, 25, 71, 47, 13),
        (0, 111, 71, 85, 47, 47, 83, 84, 70),
        (1, 17742, 17742, 87115, 9775, 17742, 15943, 9775, 76064),
        (1, 219409, 72209, 5920, 76064, 72209, 72209, 76064, 131915),
        (1, 134228, 227376, 223264, 133457, 233544, 233544, 133714, NONE),
        (1, NONE, 132686, 134228, NONE, 133714, 133714, NONE, NONE),
        (0, 0, 5, 3, 2, 0, 0, 0, 88),
        (0, 145, 136, 128, 104, 136, 112, 104, 146),
        (1, 86673, NONE, NONE, NONE, 32648, NONE, 24424, 12178),
        (0, 90, 90, 54, 69, 69, 54, 54, 18),
        (0, 126, 118, 90, 90, 90, 90, 85, 54),
        (1, 30078, 90970, 135770, 90970, 90970, 11574, 11574, 30006),
        (1, 72538, 28022, 11574, 15429, 74265, 90970, 78120, 219666),
        (1, 70996, 5920, 76064, 72209, 5920, 76064, 16971, 72466),
        (1, 3864, NONE, 7976, NONE, NONE, 26480, NONE, 78120),
        (0, 91, 91, 39, 39, 70, 46, 38, 19),
        (0, 110, 126, 91, 91, 91, 84, 86, 46),
        (1, 140910, 91227, 91227, 136027, 91227, 221208, 7462, 27950),
        (1, 225320, 30078, 225320, 225320, 219152, 78120, 224806, 229432),
        (1, 72795, 229432, 134485, 133714, 7719, 9518, 17228, 70410),
        (1, 5920, 133457, 15686, 7719, 133971, 133971, 89171, 132172),
        (1, NONE, NONE, 78120, NONE, NONE, NONE, 133971, NONE),
        (0, 1, 1, 0, 0, 1, 1, 1, 96),
        (0, 146, 144, 136, 120, 127, 136, 96, 148),
        (1, 86930, NONE, NONE, NONE, NONE, NONE, NONE, 8084),
        (0, 25, 31, 38, 25, 33, 62, 68, 20),
        (0, 118, 92, 92, 46, 46, 85, 87, 62),
        (1, 28022, 136284, 68611, 74265, 226862, 32648, 17485, 70924),
        (1, 15943, 87372, 7719, 9518, 9775, 89171, 231488, 231488),
        (1, 227376, 7976, 227376, 133971, 76321, 227119, 134228, 132429),
        (1, 135770, 231231, 136027, NONE, 221208, 135770, NONE, NONE),
        (1, NONE, 133714, NONE, NONE, 135770, NONE, NONE, NONE),
        (0, 2, 2, 1, 1, 2, 2, 2, 104),
        (0, 88, 88, 119, 128, 112, 135, 120, 147),
        (1, 72024, NONE, NONE, NONE, NONE, NONE, NONE, 10131),
        (0, 33, 25, 46, 33, 34, 31, 25, 11),
        (0, 102, 39, 93, 54, 54, 86, 69, 31),
        (1, NONE, 74265, 7462, 228918, 15429, 13630, 74265, 223007),
        (1, NONE, 15686, NONE, 76321, 76578, NONE, 17742, 71181),
        (1, NONE, 69125, NONE, 78120, NONE, NONE, NONE, NONE),
        (0, 41, 33, 17, 62, 61, 55, 33, 14),
        (0, 119, 67, 66, 92, 84, 87, 70, 89),
        (1, 229432, 76321, 72209, 13630, 223264, 225063, 76321, 15961),
        (1, 16714, 227119, 229175, 229175, 136027, 32391, 233544, 233544),
        (1, 145022, 135770, 136284, 134228, 15686, 134228, 18256, 72723),
        (1, NONE, 15943, 9518, NONE, 87372, NONE, 134485, 132686),
        (0, 3, 4, 2, 3, 3, 3, 3, 112),
        (0, 144, 96, 144, 136, 120, 104, 128, 145),
        (1, 86416, NONE, NONE, NONE, NONE, NONE, NONE, 14225),
        (0, 99, 86, 99, 38, 62, 91, 18, 45),
        (0, 117, 117, 109, 99, 99, 127, 45, 82),
        (1, 142709, 27765, 16971, 7462, 93283, 80176, 226605, 27693),
        (1, 16971, 5663, 231231, 16971, 11574, 30335, 72466, 72980),
        (1, 221465, 80176, 136541, 231231, 231231, 228918, 22368, 22296),
        (1, 136027, 229175, NONE, 135770, 134228, 134485, 219152, 231231),
        (1, NONE, 136027, NONE, NONE, NONE, NONE, 134742, 132943),
        (0, 4, 0, 4, 4, 4, 4, 4, 0),
        (0, 96, 104, 88, 144, 128, 120, 135, 90),
        (1, 74080, NONE, NONE, NONE, NONE, NONE, NONE, 16128),
        (0, 100, 68, 25, 45, 68, 33, 26, 27),
        (0, 109, 93, 117, 100, 85, 67, 30, 95),
        (1, 69454, 68097, 74265, 226605, 78120, 76321, 74522, 88914),
        (1, 1808, 7719, 17228, 17228, 13373, 5920, 15172, 24352),
        (1, NONE, NONE, NONE, NONE, NONE, 82232, NONE, NONE),
        (0, 47, 100, 33, 41, 31, 26, 27, 38),
        (0, 49, 109, 68, 68, 86, 68, 61, 83),
        (1, 9775, 223007, 76321, 78377, 225063, 74522, 74779, 229175),
        (1, 223521, 16714, 228918, 227119, 82232, 223007, 227119, 74779),
        (1, 74851, 68354, 138083, 136284, 138083, 7976, 28536, 24095),
        (1, 24167, 134742, 3864, 3864, 13630, 87886, 80176, 155974),
        (1, 142966, NONE, NONE, NONE, NONE, 134742, 134999, NONE),
        (0, 5, 11, 5, 5, 5, 5, 5, 120),
        (0, 104, 112, 96, 96, 118, 128, 111, 151),
        (1, 76136, NONE, NONE, NONE, NONE, NONE, NONE, NONE),
        (0, 26, 69, 41, 23, 26, 41, 41, 25),
        (0, 31, 84, 69, 26, 38, 69, 62, 29),
        (1, 75108, 89428, 78377, 74522, 74522, 16971, 82232, 89171),
        (1, 26223, 17228, 28279, 5920, 16971, 89428, 15429, 25894),
        (1, 225577, 68868, 225063, 225063, 87629, 134999, 222750, 218124),
        (1, 138854, 225063, 140653, 138083, 227119, NONE, NONE, 156222),
        (1, NONE, NONE, NONE, NONE, 134485, NONE, NONE, NONE),
        (0, 6, NONE, 9, 6, 6, 6, 6, 103),
        (0, 89, NONE, 104, 126, 144, 144, 110, 150),
        (1, 72281, 142709, NONE, NONE, NONE, NONE, NONE, NONE),
        (0, 34, 13, 23, 31, 41, 23, 49, 21),
        (0, 39, 120, 26, 34, 60, 49, 103, 66),
        (1, 25966, NONE, 74522, 76578, 30335, 220951, 15686, 1943),
        (1, NONE, NONE, NONE, NONE, 87886, 17228, 88143, 74265),
        (1, NONE, NONE, NONE, NONE, NONE, 89685, NONE, NONE),
        (0, 42, 15, NONE, NONE, 30, 30, 19, 28),
        (0, 108, 41, NONE, NONE, 49, 92, 37, 67),
        (1, 227633, 70667, 14658, 80176, 228918, 222750, 224549, 218381),
        (1, 138083, 1808, NONE, 24424, 9518, 11831, 30592, 23581),
        (1, 28279, NONE, NONE, NONE, 88143, 91227, 89428, 80176),
        (1, NONE, NONE, NONE, NONE, 134742, 136027, NONE, 131401),
        (0, 38, 23, 34, 61, 7, 7, 7, 128),
        (0, 112, 49, 108, 108, 88, 96, 117, 149),
        (1, 78192, 218895, 76578, 226862, NONE, NONE, NONE, NONE),
        (0, 62, NONE, NONE, NONE, 37, 34, 21, 68),
        (0, 85, NONE, NONE, NONE, 92, 38, 127, 81),
        (1, 71253, 71181, 224806, 11574, 15172, 24424, 32391, 3990),
        (1, 27765, 136541, 15172, 138340, 89428, 78377, 89685, 82232),
        (1, 221722, 3864, 142709, 87629, 223007, 224806, 220437, 219923),
        (1, 138340, NONE, 80176, NONE, NONE, NONE, NONE, 137055),
        (0, 9, 3, 18, 19, 9, 9, 9, 2),
        (0, 120, 128, 112, 112, 96, 119, 136, 136),
        (1, 80248, NONE, NONE, NONE, NONE, NONE, NONE, NONE),
        (0, 14, 12, 31, 30, 42, 42, 22, 33),
        (0, 55, 62, 42, 42, 53, 60, 53, 69),
        (1, 5663, 14915, 78634, 78634, 89685, 80433, 78377, 70667),
        (1, NONE, NONE, NONE, NONE, 5663, 14915, 13373, 6037),
        (0, 63, NONE, NONE, NONE, 29, 27, 28, 41),
        (0, 93, NONE, NONE, NONE, 35, 61, 126, 71),
        (1, 73309, 78377, 15429, 15172, 224806, 221979, 220694, 220180),
        (1, 223778, 220951, 90970, 87886, 78377, 15172, 26223, 90970),
        (1, 140653, 138340, 226862, 220951, 28022, 91484, 80433, 16642),
        (1, 7719, NONE, 140396, 140396, NONE, NONE, NONE, NONE),
        (0, 12, 20, 10, 7, 10, 10, 10, 3),
        (0, 128, 135, 120, 117, 104, 111, 144, 144),
        (1, 82304, NONE, NONE, NONE, NONE, NONE, NONE, NONE),
        (0, 57, 26, 49, 29, 57, 35, 29, 26),
        (0, 87, 38, 61, 43, 66, 45, 118, 87),
        (1, 7462, 15172, 72466, 78891, 7462, 76578, 72723, 94311),
        (1, 225834, 80433, 3607, 30078, 80433, 15429, 13630, 16899),
        (1, 140396, NONE, NONE, 68354, 222750, 226605, 222236, 218638),
        (0, 45, 34, 50, 37, 11, 11, 11, 4),
        (0, 97, 65, 62, 85, 135, 126, 88, 135),
        (1, 74337, 15429, 220951, 223007, NONE, NONE, NONE, NONE),
        (1, NONE, 70924, 5663, 91227, NONE, NONE, NONE, NONE),
        (1, NONE, 140653, 80433, 5663, NONE, NONE, NONE, NONE),
        (0, 10, 6, 12, 9, 65, 36, 23, 15),
        (0, 95, 119, 127, 127, 67, 52, 91, 59),
        (1, 13630, NONE, NONE, NONE, 13116, 78634, 91227, 88657),
        (1, NONE, NONE, NONE, NONE, 91484, 13116, 25966, 17156),
        (0, 11, 42, 22, 35, 15, 53, 31, 36),
        (0, 94, 66, 35, 66, 87, 57, 36, 111),
        (1, 231488, 72980, 13373, 91484, 224549, 224292, 222493, 221979),
        (1, 11831, 1551, 80690, 13373, 78634, 74779, 24167, 76321),
        (1, NONE, NONE, 223007, 222750, NONE, NONE, NONE, NONE),
        (0, 18, 9, 13, 10, NONE, NONE, 12, 5),
        (0, 105, 127, 135, 135, NONE, NONE, 119, 127),
        (1, 76393, NONE, NONE, NONE, 5406, 13373, NONE, 17413),
        (0, 13, 7, 30, 49, 18, 18, 66, 37),
        (0, 101, 50, 43, 67, 111, 103, 92, 60),
        (1, 13887, 3607, 13630, 72723, NONE, NONE, 91484, 78377),
        (1, 218638, 74522, 76835, 5406, NONE, NONE, 27765, 224806),
        (1, NONE, NONE, NONE, NONE, NONE, NONE, 224292, NONE),
        (0, 54, 35, 51, 15, 23, 65, 13, 6),
        (0, 113, 94, 65, 65, 93, 66, 102, 84),
        (1, 78449, 76578, 222750, 224549, 11317, 76835, NONE, 17670),
        (1, NONE, NONE, 3350, 27765, NONE, NONE, NONE, NONE),
        (0, 7, NONE, NONE, NONE, NONE, NONE, 34, 49),
        (0, 20, NONE, NONE, NONE, NONE, NONE, 67, 61),
        (1, 9261, 13630, 78891, 89685, 76835, 11060, 76578, 74522),
        (0, 22, 10, 19, 11, 19, 12, NONE, 22),
        (0, 92, 103, 126, 119, 119, 95, NONE, 119),
        (1, NONE, NONE, NONE, NONE, NONE, NONE, 30335, 220437),
        (0, 19, 43, 52, 86, 94, 88, 46, 7),
        (0, 121, 102, 67, 110, 95, 118, 57, 85),
        (1, 80505, 7462, 5406, 5149, 5149, 11317, 11317, 17927),
        (1, NONE, 78634, 80947, 76835, NONE, NONE, NONE, NONE),
        (0, 15, 18, 20, 12, 45, 37, 14, 57),
        (0, 50, 111, 111, 111, 100, 93, 109, 126),
        (1, NONE, NONE, NONE, NONE, NONE, NONE, NONE, 222236),
        (0, 46, 51, 7, 57, 12, 13, 65, 91),
        (0, 98, 101, 57, 87, 126, 102, 95, 97),
        (1, 74594, 80690, 81204, 7205, NONE, NONE, 30078, 15713),
        (0, 23, 57, 15, 59, 50, 59, 15, 30),
        (0, 58, 110, 86, 88, 59, 94, 93, 52),
        (1, NONE, 76835, NONE, NONE, NONE, NONE, NONE, NONE),
        (0, 21, 19, 21, 18, 27, 14, 20, 65),
        (0, 65, 87, 110, 118, 103, 110, 58, 102),
        (0, 30, 99, 58, 60, 58, 22, NONE, 92),
        (0, 106, 108, 87, 93, 117, 50, NONE, 98),
        (1, 76650, 78891, NONE, NONE, NONE, NONE, 28022, 13666),
        (0, 29, 14, 27, 20, 22, 58, 59, 34),
        (0, 66, 95, 118, 95, 101, 109, 99, 53),
        (0, 27, 22, 11, 14, 13, 15, 94, 1),
        (0, 114, 27, 59, 94, 110, 99, 60, 86),
        (1, 78706, 80947, NONE, NONE, NONE, NONE, NONE, NONE),
        (0, 35, 30, 60, 22, 43, 28, 112, 42),
        (0, 67, 58, 100, 50, 52, 29, 100, 101),
        (0, 43, 45, 37, 27, 14, 19, 51, 50),
        (0, 68, 29, 95, 103, 102, 117, 90, 94),
        (0, 28, 59, 6, 52, 21, 51, 42, 23),
        (0, 136, 21, 101, 58, 51, 100, 52, 99),
        (0, 51, 44, 45, 28, 36, 21, 101, 58),
        (0, 69, 53, 103, 102, 108, 101, 43, 108),
        (0, 37, 46, 14, 53, 109, 108, 50, 110),
        (0, 86, 52, 28, 101, 20, 43, 108, 35),
        (0, 59, 28, 53, 13, 44, 44, 35, 118),
        (0, 70, 54, 94, 51, 28, 20, 44, 43),
        (0, 44, 60, 36, 36, NONE, NONE, NONE, 44),
        (0, 61, 37, 102, 109, NONE, NONE, NONE, 93),
        (0, 36, 36, 29, 21, NONE, NONE, NONE, 51),
        (0, 52, 61, 44, 44, NONE, NONE, NONE, 117),
        (0, 53, NONE, NONE, NONE, NONE, NONE, NONE, 100),
        (0, 60, NONE, NONE, NONE, NONE, NONE, NONE, 109),
    ),
    (
        (1, 16200, 14144, 14144, 86344, 86344, 86344, 86344, 32576),
        (1, 67912, 86344, 86344, 16200, 16200, 16200, 16200, 86344),
        (1, 131144, 132429, 131915, 131658, 131144, 131144, 131144, 168504),
        (1, 69968, 16200, 16200, 14144, 12088, 14144, 12088, 34632),
        (1, 12088, 86601, 86601, 86601, 86601, 86601, 86601, 86601),
        (1, 131401, 131401, 131144, 131144, 131401, 131401, 131401, 169000),
        (1, 68169, 86858, 86858, 86858, 10032, 86858, 14144, 18184),
        (1, 14144, 18256, 17999, 18256, 86858, 18256, 71952, 69896),
        (1, 68683, 69896, 87372, 10032, 87115, 10032, 10032, 26408),
        (1, 17999, 12088, 18256, 87115, 17999, 69896, 69896, 86858),
        (1, 131658, 131658, 131401, 131401, 131658, 131658, 131658, 168752),
        (1, 68940, 87115, 12088, 12088, 18256, 12088, 86858, 28464),
        (1, 18256, 17999, 69896, 87372, 69896, 71952, 17999, 87115),
        (1, 131915, 132172, 131658, 131915, 131915, 131915, 131915, 168256),
        (1, 132172, 10032, 17742, 17742, 132172, 132172, 87115, 87372),
        (1, 7976, 131144, 10032, 17999, 71952, 17485, 132172, 87629),
        (1, 132429, 71952, 132172, 132172, 132429, 74008, 87372, 131144),
        (1, 68426, 74008, 132429, 132429, 7976, 132429, 132429, 87886),
        (1, 10032, NONE, 71952, NONE, 74008, 17742, 7976, 169744),
        (1, NONE, NONE, NONE, NONE, NONE, NONE, 87629, 71952),
        (0, 81, 63, 55, 55, 63, 63, 63, 9),
        (0, 127, 81, 81, 81, 81, 81, 81, 63),
        (1, 70225, 13887, 88657, 88657, 13887, 13887, 13887, 32319),
        (1, 30335, 88657, 11831, 11831, 88657, 88657, 88657, 74008),
        (1, 17228, 16971, 74008, 69896, 14144, 87115, 87886, 30520),
        (1, 69197, 76064, 133457, 132686, 132686, 17999, 22792, 169496),
        (1, 132686, NONE, NONE, NONE, NONE, 132686, 132686, NONE),
        (0, 82, 47, 63, 63, 55, 47, 55, 17),
        (0, 135, 82, 82, 82, 82, 82, 82, 47),
        (1, 70482, 88914, 88914, 88914, 11831, 9775, 11831, 28207),
        (1, 32391, 9775, 13887, 13887, 88914, 88914, 88914, 70153),
        (1, NONE, 131915, 87629, NONE, 132943, 132943, 132943, 169248),
        (0, 71, 55, 71, 70, 71, 25, 17, 10),
        (0, 83, 83, 83, 83, 83, 39, 71, 55),
        (1, 70739, 133971, 89171, 89171, 15943, 74265, 15943, 30263),
        (1, 17485, 11831, 15943, 15686, 89171, 7719, 74008, 72209),
        (1, NONE, NONE, NONE, 17485, 17228, 87372, NONE, NONE),
        (1, NONE, NONE, NONE, 71952, NONE, NONE, NONE, NONE),
        (0, 17, 70, 47, 71, 17, 17, 39, 12),
        (0, 103, 85, 84, 84, 39, 70, 83, 39),
        (1, 133457, 134485, 9775, 89428, 17485, 15686, 72209, 26151),
        (1, NONE, 17485, 89428, 15943, 76064, 87629, 133457, 131658),
        (1, NONE, 78120, 17485, 74008, 133457, 133457, NONE, NONE),
        (1, NONE, NONE, 133714, 7976, NONE, NONE, NONE, NONE),
        (1, NONE, NONE, NONE, 132943, NONE, NONE, NONE, NONE),
        (0, 84, 17, 70, 17, 25, 71, 47, 13),
        (0, 111, 71, 85, 47, 47, 83, 84, 70),
        (1, 17742, 17742, 87115, 9775, 17742, 15943, 9775, 76064),
        (1, 134228, 72209, 5920, 76064, 72209, 72209, 76064, 131915),
        (1, NONE, 132686, 134228, 133457, 133714, 133714, 133714, NONE),
        (0, 145, 136, 128, 104, 136, 112, 104, 88),
        (1, 86673, NONE, NONE, NONE, 32648, NONE, 24424, NONE),
        (0, 90, 90, 54, 69, 69, 54, 54, 18),
        (0, 126, 118, 90, 90, 90, 90, 85, 54),
        (1, 30078, 90970, 135770, 90970, 90970, 11574, 11574, 30006),
        (1, 72538, 28022, 11574, 15429, 74265, 90970, 78120, 72466),
        (1, 70996, 5920, 76064, 72209, 5920, 76064, 16971, 78120),
        (1, 3864, NONE, 7976, NONE, NONE, 26480, NONE, NONE),
        (0, 91, 91, 39, 39, 70, 46, 38, 19),
        (0, 110, 126, 91, 91, 91, 84, 86, 46),
        (1, 140910, 91227, 91227, 136027, 91227, 78120, 7462, 27950),
        (1, 72795, 30078, 15686, 7719, 7719, 9518, 17228, 70410),
        (1, 5920, 133457, 78120, 133714, 133971, 133971, 89171, 132172),
        (1, NONE, NONE, 134485, NONE, NONE, NONE, 133971, NONE),
        (0, 146, 144, 136, 120, 127, 136, 96, 96),
        (1, 86930, NONE, NONE, NONE, NONE, NONE, NONE, NONE),
        (0, 25, 31, 38, 25, 33, 62, 68, 20),
        (0, 118, 92, 92, 46, 46, 85, 87, 62),
        (1, 28022, 136284, 7719, 74265, 9775, 32648, 17485, 70924),
        (2,),
        (1, 15943, 87372, 229432, 9518, 76321, 89171, 223264, 219152),
        (1, 233801, 7976, NONE, 223264, 231488, 225320, NONE, NONE),
        (1, NONE, 231488, NONE, NONE, NONE, NONE, NONE, NONE),
        (0, 0, 5, 3, 2, 0, 0, 0, 146),
        (1, 135770, 133714, 68611, 133971, 135770, 135770, 134228, 12178),
        (1, NONE, NONE, 136027, NONE, NONE, NONE, NONE, 132429),
        (0, 88, 88, 119, 128, 112, 135, 120, 104),
        (1, 72024, NONE, NONE, NONE, NONE, NONE, NONE, NONE),
        (0, 33, 25, 46, 33, 34, 31, 25, 11),
        (0, 102, 39, 93, 54, 54, 86, 69, 31),
        (1, NONE, 74265, 7462, 76321, 15429, 13630, 74265, 71181),
        (1, NONE, 15686, NONE, 78120, 76578, NONE, 17742, NONE),
        (0, 41, 33, 17, 62, 61, 55, 33, 14),
        (0, 119, 67, 66, 92, 84, 87, 70, 89),
        (1, 234058, 76321, 72209, 13630, 229175, 231488, 76321, 15961),
        (1, NONE, 233544, 231488, 227376, NONE, NONE, 221208, 221208),
        (0, 1, 1, 0, 0, 1, 1, 1, 148),
        (1, 16714, 68097, 9518, 134228, 15686, 32391, 18256, 8084),
        (1, 145022, 15943, 136284, NONE, 87372, 134228, 134485, 72723),
        (1, NONE, 135770, NONE, NONE, 136027, NONE, NONE, 132686),
        (0, 144, 96, 144, 136, 120, 104, 128, 112),
        (1, 86416, NONE, NONE, NONE, NONE, NONE, NONE, NONE),
        (0, 99, 86, 99, 38, 62, 91, 18, 45),
        (0, 117, 117, 109, 99, 99, 127, 45, 82),
        (1, 142709, 27765, 16971, 7462, 93283, 80176, 72466, 27693),
        (1, 16971, 5663, 227119, 16971, 11574, 30335, 22368, 72980),
        (1, 219152, 80176, NONE, 229432, 225320, 231231, 227376, 22296),
        (1, NONE, 219152, NONE, NONE, NONE, NONE, NONE, 223264),
        (0, 2, 2, 1, 1, 2, 2, 2, 147),
        (1, 136027, 136027, 136541, 135770, 134228, 134485, 134742, 10131),
        (1, NONE, NONE, NONE, NONE, NONE, NONE, NONE, 132943),
        (0, 96, 104, 88, 144, 128, 120, 135, 90),
        (1, 74080, NONE, NONE, NONE, NONE, NONE, NONE, NONE),
        (0, 100, 68, 25, 45, 68, 33, 26, 27),
        (0, 109, 93, 117, 100, 85, 67, 30, 95),
        (1, 69454, 7719, 74265, 17228, 78120, 76321, 74522, 88914),
        (1, 1808, 68354, 17228, NONE, 13373, 5920, 15172, 24352),
        (1, NONE, NONE, NONE, NONE, NONE, 82232, NONE, NONE),
        (0, 47, 100, 33, 41, 31, 26, 27, 38),
        (1, 9775, NONE, NONE, NONE, NONE, NONE, NONE, NONE),
        (0, 49, 109, 68, 68, 86, 68, 61, 83),
        (1, 233544, 221208, 76321, 78377, 227376, 74522, 74779, 225320),
        (1, NONE, NONE, 233544, 231488, NONE, 223264, 229432, NONE),
        (0, 3, 4, 2, 3, 3, 3, 3, 145),
        (1, 74851, 16714, 3864, 3864, 82232, 7976, 28536, 14225),
        (1, 24167, 68868, 138083, 136284, 13630, 87886, 80176, 74779),
        (1, 142966, 134742, NONE, NONE, 138083, 134742, 134999, 24095),
        (1, NONE, NONE, NONE, NONE, NONE, NONE, NONE, 155974),
        (0, 104, 112, 96, 96, 118, 128, 111, 120),
        (1, 76136, NONE, NONE, NONE, NONE, NONE, NONE, NONE),
        (0, 26, 69, 41, 23, 26, 41, 41, 25),
        (0, 31, 84, 69, 26, 38, 69, 62, 29),
        (1, 75108, 89428, 78377, 74522, 74522, 16971, 82232, 89171),
        (1, 26223, 17228, 28279, 5920, 16971, 89428, 15429, 25894),
        (1, 221208, 69125, 219152, 233544, 87629, 227376, 231231, 219666),
        (1, NONE, NONE, NONE, NONE, 229432, NONE, NONE, NONE),
        (0, 4, NONE, 4, 4, 4, 4, 4, 0),
        (1, 138854, 223264, 140653, 138083, 134485, 134999, NONE, 156222),
        (0, 89, 0, 104, 126, 144, 144, 110, 103),
        (1, 72281, 142709, NONE, NONE, NONE, NONE, NONE, NONE),
        (0, 34, 120, 23, 31, 41, 23, 49, 21),
        (0, NONE, NONE, NONE, NONE, 60, 49, 103, 66),
        (1, 25966, NONE, NONE, NONE, 30335, 17228, 15686, 74265),
        (1, NONE, NONE, NONE, NONE, 87886, 89685, 88143, 16128),
        (0, 42, 15, 26, 34, 30, 30, 19, 28),
        (0, 108, 41, NONE, NONE, 49, 92, 37, 67),
        (1, 223264, 1808, 74522, 76578, 226862, 229432, 225063, 227376),
        (0, 5, 23, NONE, NONE, 5, 5, 5, 151),
        (1, 28279, NONE, 14658, 80176, 9518, 11831, 30592, 23581),
        (1, 138083, NONE, NONE, 24424, 88143, 91227, 89428, 80176),
        (0, 112, 49, 34, 61, NONE, NONE, NONE, NONE),
        (0, NONE, NONE, 108, 108, NONE, NONE, NONE, NONE),
        (1, 78192, 225320, 76578, 221208, 134742, 136027, NONE, 131401),
        (1, NONE, NONE, 221208, NONE, NONE, NONE, NONE, NONE),
        (0, 62, 11, 5, 5, 88, 96, 117, 128),
        (0, 85, NONE, NONE, NONE, 37, 34, 21, 68),
        (0, NONE, NONE, NONE, NONE, 92, 38, 127, 81),
        (1, 71253, 70667, 15172, 11574, 15172, 24424, 32391, 82232),
        (1, 27765, 3864, 80176, 87629, 89428, 78377, 89685, 1943),
        (1, 219409, 136541, 142709, 138340, 233544, 233544, 224806, 223007),
        (0, 6, 128, 112, 112, 6, 6, 6, 150),
        (1, NONE, NONE, NONE, NONE, NONE, NONE, NONE, 137055),
        (0, 10, 12, 31, 30, 96, 119, 136, 136),
        (0, 39, NONE, 42, 42, 42, 42, 22, 33),
        (1, 138340, 70924, 78634, 78634, NONE, NONE, NONE, NONE),
        (0, 120, 62, NONE, NONE, 53, 60, 53, 69),
        (1, 80248, 14915, 15429, 15172, 89685, 80433, 78377, 70667),
        (1, 5663, 78377, 90970, 87886, 5663, 14915, 13373, 3990),
        (0, 55, NONE, NONE, NONE, 29, 27, 28, 41),
        (0, 93, NONE, NONE, NONE, 35, 61, 126, 71),
        (1, 73309, 227376, 223264, 228918, 219152, 221208, 226605, 229432),
        (1, 225320, NONE, NONE, NONE, NONE, NONE, NONE, NONE),
        (0, 38, 13, 9, 6, 7, 7, 7, 149),
        (1, 7462, NONE, 140396, 140396, 78377, 15172, 26223, 90970),
        (1, 140653, NONE, NONE, NONE, 28022, 91484, 80433, 6037),
        (0, 128, 38, 120, 117, 104, 111, 144, 144),
        (1, 82304, 138340, NONE, NONE, NONE, NONE, NONE, NONE),
        (0, 57, 135, 49, 29, 57, 35, 29, 26),
        (0, 87, 26, 61, 43, 66, 45, 118, 87),
        (1, 7719, 15172, 3607, 78891, 7462, 76578, 72723, 94311),
        (1, 227376, 80433, NONE, 30078, 80433, 15429, 13630, 231488),
        (1, NONE, NONE, NONE, 68354, 221208, 227119, 231488, NONE),
        (0, 9, 34, 50, 37, 9, 9, 9, 2),
        (0, 11, 65, 62, 85, NONE, NONE, NONE, NONE),
        (1, 140396, 229432, 225320, 225320, NONE, NONE, NONE, 16642),
        (0, 97, 3, 18, 19, 135, 126, 88, 135),
        (1, 74337, 15429, 72466, 91227, NONE, NONE, NONE, NONE),
        (1, NONE, NONE, 5663, 5663, NONE, NONE, NONE, NONE),
        (0, 95, NONE, NONE, NONE, 65, 36, 23, 15),
        (1, 13630, 71181, 80433, NONE, NONE, NONE, NONE, NONE),
        (0, 13, NONE, 127, 127, 67, 52, 91, 59),
        (0, 94, NONE, 22, 35, NONE, NONE, NONE, NONE),
        (1, 229432, 140653, NONE, NONE, 13116, 78634, 91227, 88657),
        (0, 12, 119, 35, 66, NONE, NONE, NONE, NONE),
        (0, 105, 42, NONE, NONE, NONE, NONE, NONE, NONE),
        (1, 76393, NONE, 13373, 91484, 91484, 13116, 25966, NONE),
        (0, 14, 66, NONE, NONE, 15, 53, 31, 36),
        (0, 101, NONE, NONE, NONE, 87, 57, 36, 111),
        (1, 11831, 1551, 80690, 13373, 223264, 225063, 233544, 233544),
        (1, 221465, 231231, 227376, 226605, NONE, NONE, NONE, NONE),
        (0, 45, 20, 10, 7, 10, 10, 10, 3),
        (1, 9261, 72980, NONE, NONE, 78634, 74779, 24167, 16899),
        (1, NONE, NONE, NONE, NONE, 5406, 13373, NONE, 76321),
        (0, 20, 127, 135, 135, 111, 103, 119, 127),
        (0, 63, 7, 30, 49, 23, 65, 66, 37),
        (0, 113, 50, 43, 67, 93, 66, 92, 60),
        (1, 78449, 3607, 13630, 5406, 11317, 76835, 91484, 78377),
        (1, 13887, 74522, 76835, 72723, 76835, 11060, 27765, 231231),
        (0, 21, 35, 51, 15, NONE, NONE, NONE, 4),
        (0, 92, 94, 65, 65, NONE, NONE, NONE, NONE),
        (1, 223521, 227119, 229175, 229175, 231231, 228918, 219152, 17156),
        (0, 18, 6, 12, 9, 11, 11, 11, 84),
        (0, 121, NONE, NONE, NONE, 119, 95, 102, 49),
        (0, NONE, NONE, NONE, NONE, 94, 88, 34, 61),
        (1, 80505, 76578, 3350, 27765, NONE, NONE, NONE, 74522),
        (0, 7, NONE, NONE, NONE, 95, 118, 67, 22),
        (0, 50, NONE, NONE, NONE, NONE, NONE, NONE, 119),
        (1, 225577, 13630, 78891, 89685, 5149, 11317, 76578, 229175),
        (0, 54, 103, 126, 119, 45, 37, NONE, 5),
        (1, NONE, NONE, NONE, NONE, NONE, NONE, 30335, 17413),
        (0, 15, 43, 52, 86, 100, 93, 46, 85),
        (0, 98, 102, 67, 110, NONE, NONE, 57, 57),
        (1, 74594, 78634, 5406, 5149, NONE, NONE, NONE, NONE),
        (1, NONE, 7462, 80947, 76835, NONE, NONE, NONE, NONE),
        (0, NONE, NONE, NONE, NONE, NONE, NONE, NONE, 126),
        (1, NONE, 229175, 231231, 231231, 225063, 223007, 227119, 218124),
        (0, 58, 9, 13, 10, 18, 18, 12, 6),
        (1, NONE, NONE, NONE, NONE, NONE, NONE, 11317, 17670),
        (0, 22, 111, 111, 111, 126, 102, 109, 91),
        (0, 23, 51, 7, 57, 50, 59, 65, 30),
        (0, NONE, 101, 57, 87, 59, 94, 95, 52),
        (1, 227633, 80690, 81204, 7205, NONE, NONE, NONE, NONE),
        (0, 19, 57, 15, 59, NONE, NONE, NONE, 65),
        (0, 106, 110, 86, 88, NONE, NONE, NONE, 102),
        (1, 76650, 223007, 228918, 227119, 227119, 220951, 30078, 218381),
        (0, 29, 10, 19, 11, 19, 12, NONE, 7),
        (0, 65, NONE, 110, 118, NONE, NONE, NONE, NONE),
        (1, 221722, 76835, NONE, NONE, NONE, NONE, 222750, 17927),
        (0, 46, 87, 58, 60, 103, 110, 13, 92),
        (0, 66, 99, 87, 93, 58, 22, 93, 34),
        (0, 114, 108, NONE, NONE, 117, 50, 20, 53),
        (1, 78706, 78891, 225063, 225063, NONE, NONE, NONE, 219923),
        (1, NONE, 225063, NONE, NONE, NONE, NONE, NONE, NONE),
        (0, 35, 18, 20, 12, 22, 58, 58, 97),
        (1, NONE, NONE, NONE, NONE, NONE, NONE, 28022, 15713),
        (0, 67, 22, 11, 95, 101, 109, 59, 86),
        (0, 43, 27, 118, 14, NONE, NONE, 99, 42),
        (0, NONE, 95, 59, 94, NONE, NONE, NONE, 101),
        (1, 223778, 80947, NONE, NONE, NONE, NONE, NONE, NONE),
        (0, 30, 29, 60, 22, NONE, NONE, NONE, 50),
        (0, 136, 58, 100, 50, NONE, NONE, NONE, 94),
        (1, NONE, 218895, 224806, 226862, 228918, 222750, 224549, 220180),
        (0, 68, 19, 21, 18, 12, 13, 14, 98),
        (1, NONE, NONE, NONE, NONE, NONE, NONE, NONE, 13666),
        (0, 51, 30, 95, 103, 110, 99, 94, 99),
        (0, NONE, 59, 6, 52, 43, 28, 60, 58),
        (0, NONE, NONE, 101, 58, 52, 29, 112, 108),
        (1, 225834, 220951, 226862, 220951, 223007, 224806, 220437, 218638),
        (0, 27, 14, 27, 20, 27, 14, 15, 1),
        (0, 69, 44, 28, 102, 102, 117, 100, 110),
        (0, 86, 53, 103, 53, 21, 51, 51, 35),
        (0, 59, 36, 14, 101, 51, 100, 90, 118),
        (0, 61, 52, 53, 13, 36, 21, 42, 43),
        (0, 44, 45, 94, 51, 108, 101, 52, 44),
        (1, 231488, NONE, 220951, 223007, 224806, 221979, 220694, 221979),
        (0, 28, 46, 37, 27, 13, 15, 101, 23),
        (0, 70, 60, 102, 109, 109, 108, 43, 93),
        (0, 52, 21, 29, 21, 20, 43, 50, 51),
        (0, NONE, NONE, 44, 44, NONE, NONE, NONE, NONE),
        (1, 218638, NONE, 223007, 222750, NONE, NONE, 222236, NONE),
        (0, 37, 54, 45, 28, 44, 44, 108, 117),
        (1, NONE, NONE, 222750, 224549, 222750, 226605, NONE, 224806),
        (0, 53, 61, 36, 36, 14, 19, 35, 100),
        (0, 60, 28, NONE, NONE, 28, 20, 44, 109),
        (1, NONE, NONE, NONE, NONE, 224549, 224292, 222493, 220437),
        (0, 36, 37, NONE, NONE, NONE, NONE, NONE, NONE),
        (1, NONE, NONE, NONE, NONE, NONE, NONE, 224292, 222236),
    ),
)
OWN = BAND * HALF


def device_of(row, cols):
    return row // cols, lax.rem(row, cols)


def kernel(cols_hbm, blocks_hbm, out_ref, cols_ref, blocks_ref, own, square, upper, flipped, newband, in_sem, entered, send_sem, recv_sem):
    size = blocks_ref.shape[-1]
    loads = [
        pltpu.make_async_copy(cols_hbm, cols_ref, in_sem.at[0]),
        pltpu.make_async_copy(blocks_hbm, blocks_ref, in_sem.at[1]),
    ]
    for load in loads:
        load.start()
    cols = lax.axis_size("col")
    count = cols * lax.axis_size("row")
    me = lax.axis_index("row") * cols + lax.axis_index("col")
    place = lax.rem(me, RING)
    start = me - place
    targets = (
        start + lax.rem(place + 1, RING),
        start + lax.rem(place + RING - 1, RING),
        lax.rem(me + RING, count),
        lax.rem(me + count - RING, count),
    )
    barrier = pltpu.get_barrier_semaphore()
    peers = [device_of(target, cols) for target in targets]
    for peer in (peers[0], peers[1], peers[3]):
        pl.semaphore_signal(barrier, inc=1, device_id=peer, device_id_type=MESH)

    bits = [lax.rem(place // 2**n, 2) == 1 for n in range(3)]

    def pick(values):
        for bit in bits:
            values = [jnp.where(bit, high, low) for low, high in zip(values[::2], values[1::2])]
        return values[0]

    for load in loads:
        load.wait()
    missing = jnp.int32(0)
    for s in range(WINDOW - 1):
        offset = lax.rem(cols_ref[0, s] - me + BAND + count, count)
        missing += jnp.where(offset == s, 1, 0)

    for o in range(WINDOW):
        first = blocks_ref[0, min(o, WINDOW - 2)]
        second = blocks_ref[0, max(o - 1, 0)]
        block = jnp.where(o < missing, first, jnp.where(o == missing, jnp.zeros_like(first), second))
        own[:, o * size : (o + 1) * size] = block
        if o >= BAND:
            upper[OWN + o - BAND] = block
        else:
            slot = o * HALF + BAND - o
            upper[slot] = block.T
            flipped[slot] = block

    pl.semaphore_wait(barrier, 3)
    pl.semaphore_signal(entered, inc=1, device_id=peers[2], device_id_type=MESH)

    def copy(here, there, peer):
        return pltpu.make_async_remote_copy(
            src_ref=upper.at[here],
            dst_ref=upper.at[there],
            send_sem=send_sem,
            recv_sem=recv_sem.at[there],
            device_id=peer,
            device_id_type=MESH,
        )

    def send(code):
        direction = code >> 16
        ahead, far = (direction & 1) == 0, direction >= 2
        peer = tuple(
            jnp.where(far, jnp.where(ahead, c, d), jnp.where(ahead, a, b)) for a, b, c, d in zip(*peers)
        )
        copy(code & 255, (code >> 8) & 255, peer).start()

    def receive(here):
        copy(here, here, peers[0]).wait_recv()

    def turn(here):
        flipped[here] = upper[here].T

    def where_any(codes, code, action):
        if NONE in codes:
            pl.when(code != NONE)(functools.partial(action, code))
        else:
            action(code)

    def exchange(events):
        unturned, sending = [], False
        for kind, *codes in events:
            code = pick([jnp.int32(c) for c in codes]) if codes else None
            if kind == 1:
                where_any(codes, code, send)
            elif kind == 2:
                pl.semaphore_wait(entered, 1)
            else:
                if sending:
                    for late in unturned:
                        where_any(*late, turn)
                    unturned = []
                where_any(codes, code, receive)
                unturned.append((codes, code))
            sending = kind == 1
        for late in unturned:
            where_any(*late, turn)

    ring = lax.rem(me // RING, 16)
    ring = jnp.where((ring == 0) | (ring == 4), 1, 0)
    sends = jnp.int32(0)
    for n, events in enumerate(EVENTS):
        pl.when(ring == n)(functools.partial(exchange, events))
        counts = [sum(e[0] == 1 and e[1 + y] != NONE for e in events) for y in range(RING)]
        sends = jnp.where(ring == n, pick([jnp.int32(c) for c in counts]), sends)
    for d in range(HALF):
        flipped[OWN + d] = upper[OWN + d].T

    def block_at(k, j):
        if abs(k - j) > BAND:
            return jnp.zeros((size, size), upper.dtype)
        return upper[k * HALF + j - k] if k <= j else flipped[j * HALF + k - j]

    def product(factor, first, width):
        low, high = max(0, first - BAND), min(WINDOW, first + width + BAND)
        columns = [
            jnp.concatenate([block_at(k, j) for k in range(low, high)], axis=0) for j in range(first, first + width)
        ]
        return jnp.dot(
            factor[:, low * size : high * size],
            jnp.concatenate(columns, axis=1),
            preferred_element_type=jnp.float32,
        )

    for first in range(0, WINDOW, 2):
        width = min(2, WINDOW - first)
        total = product(own, first, width)
        for w in range(width):
            piece = total[:, w * size : (w + 1) * size]
            piece = jnp.where(missing == first + w, 0.0, piece).astype(square.dtype)
            square[:, (first + w) * size : (first + w + 1) * size] = piece
    for first in range(0, WINDOW, 2):
        width = min(2, WINDOW - first)
        total = product(square, first, width)
        for w in range(width):
            part = slice((first + w) * size, (first + w + 1) * size)
            value = 3.0 * square[:, part].astype(jnp.float32) - 2.0 * total[:, w * size : (w + 1) * size]
            newband[first + w] = value.astype(newband.dtype)
    for s in range(WINDOW - 1):
        out_ref[0, s] = jnp.where(s < missing, newband[s], newband[s + 1])

    for number in sorted({sum(e[0] == 1 and e[1 + y] != NONE for e in events) for events in EVENTS for y in range(RING)}):
        blocks = upper.at[pl.ds(0, number)]
        pl.when(sends == number)(lambda blocks=blocks: pltpu.make_async_copy(blocks, blocks, send_sem).wait())


def per_device(block_cols, blocks):
    size = blocks.shape[-1]
    kind = blocks.dtype
    return pl.pallas_call(
        kernel,
        out_shape=jax.ShapeDtypeStruct(blocks.shape, kind),
        in_specs=[pl.BlockSpec(memory_space=pltpu.HBM)] * 2,
        out_specs=pl.BlockSpec(memory_space=pltpu.VMEM),
        scratch_shapes=[
            pltpu.SMEM(block_cols.shape, block_cols.dtype),
            pltpu.VMEM(blocks.shape, kind),
            pltpu.VMEM((size, WINDOW * size), kind),
            pltpu.VMEM((size, WINDOW * size), kind),
            pltpu.VMEM((WINDOW * HALF, size, size), kind),
            pltpu.VMEM((WINDOW * HALF, size, size), kind),
            pltpu.VMEM((WINDOW, size, size), kind),
            pltpu.SemaphoreType.DMA((2,)),
            pltpu.SemaphoreType.REGULAR,
            pltpu.SemaphoreType.DMA,
            pltpu.SemaphoreType.DMA((WINDOW * HALF,)),
        ],
        compiler_params=pltpu.CompilerParams(collective_id=0, has_side_effects=True, vmem_limit_bytes=40 * 2**20),
        cost_estimate=pl.CostEstimate(flops=4 * 217 * size**3, bytes_accessed=2 * 2**20, transcendentals=0),
        name="purify",
    )(*(pltpu.with_memory_space_constraint(x, pltpu.HBM) for x in (block_cols, blocks)))


def solution(mesh):
    placed = (P(("row", "col"), None), P(("row", "col"), None, None, None))
    return jax.shard_map(
        per_device,
        mesh=mesh,
        in_specs=placed,
        out_specs=P(("row", "col"), None, None, None),
        check_vma=False,
    )
```

time: 360 us -> 39.3 us (0.11)
  the two profiles are of different devices: /device:TPU:68 before, /device:TPU:6 now
where the time goes in v3:
time: 39.3 us; the launch traced here: 38.8 us
  Pallas kernels  38 us (97%)
  local copies, waits for them, and re-layouts  0.8 us (2%)
    pallas_call x1, Pallas kernels, per_device(): pl.pallas_call(kernel, out_shape=jax.ShapeDtypeStruct(blocks.shape, kind)...  38 us
    unnamed x1, local copies, waits for them, and re-layouts  0.8 us

profile of v3, /device:TPU:6, one launch (start us, length us, event | category | flops | bytes accessed | tf_op | source)
XLA Modules:
  0.0 38.8 jit_solution(8164240838530494384)
XLA Ops:
  0.0 38.0 %purify.1 = bf16[1,16,128,128]{3,2,1,0:T(8,128)(2,1)S(1)} custom-call(s32[1,16]{1,0:T(1,128)} %cols_hbm.1, bf16[1,16,128,128]{3,2,1,0:T(8,128)(2,1)} %blocks_hbm.1), custom_call_target="tpu_custom_call" | custom-call | flops 1820327936 | bytes 2097152 | tf_op jit(solution)/shard_map/purify/pallas_call | solution.py:702
  38.0 0.8 %copy.4 = bf16[1,16,128,128]{3,2,1,0:T(8,128)(2,1)} copy(bf16[1,16,128,128]{3,2,1,0:T(8,128)(2,1)S(1)} %purify.1) | data formatting | bytes 1048576

commit v4 on v3

--- a/solution.py
+++ b/solution.py
@@ -330,46 +330,50 @@
         (1, 3864, NONE, 7976, NONE, NONE, 26480, NONE, NONE),
         (0, 91, 91, 39, 39, 70, 46, 38, 19),
         (0, 110, 126, 91, 91, 91, 84, 86, 46),
-        (1, 140910, 91227, 91227, 136027, 91227, 78120, 7462, 27950),
-        (1, 72795, 30078, 15686, 7719, 7719, 9518, 17228, 70410),
-        (1, 5920, 133457, 78120, 133714, 133971, 133971, 89171, 132172),
-        (1, NONE, NONE, 134485, NONE, NONE, NONE, 133971, NONE),
+        (2,),
+        (1, 140910, 91227, 91227, 136027, 91227, 225320, 7462, 27950),
+        (1, 233801, 30078, 229432, 223264, 231488, NONE, 223264, 219152),
+        (1, NONE, 231488, NONE, NONE, NONE, NONE, NONE, NONE),
+        (0, 0, 5, 3, 2, 0, 0, 0, 146),
+        (1, 72795, 133457, 15686, 7719, 7719, 78120, 17228, 12178),
+        (1, 5920, NONE, 78120, 133714, 133971, 9518, 89171, 70410),
+        (1, NONE, NONE, 134485, NONE, NONE, 133971, 133971, 132172),
         (0, 146, 144, 136, 120, 127, 136, 96, 96),
         (1, 86930, NONE, NONE, NONE, NONE, NONE, NONE, NONE),
         (0, 25, 31, 38, 25, 33, 62, 68, 20),
         (0, 118, 92, 92, 46, 46, 85, 87, 62),
         (1, 28022, 136284, 7719, 74265, 9775, 32648, 17485, 70924),
-        (2,),
-        (1, 15943, 87372, 229432, 9518, 76321, 89171, 223264, 219152),
-        (1, 233801, 7976, NONE, 223264, 231488, 225320, NONE, NONE),
-        (1, NONE, 231488, NONE, NONE, NONE, NONE, NONE, NONE),
-        (0, 0, 5, 3, 2, 0, 0, 0, 146),
-        (1, 135770, 133714, 68611, 133971, 135770, 135770, 134228, 12178),
-        (1, NONE, NONE, 136027, NONE, NONE, NONE, NONE, 132429),
+        (1, 15943, 87372, 68611, 9518, 76321, 89171, 221208, 221208),
+        (1, 234058, 7976, 231488, 227376, 229175, 231488, NONE, NONE),
+        (1, NONE, 233544, NONE, NONE, NONE, NONE, NONE, NONE),
+        (0, 1, 1, 0, 0, 1, 1, 1, 148),
+        (1, 135770, 133714, 136027, 133971, 135770, 135770, 134228, 8084),
+        (1, NONE, NONE, NONE, NONE, NONE, NONE, NONE, 132429),
         (0, 88, 88, 119, 128, 112, 135, 120, 104),
         (1, 72024, NONE, NONE, NONE, NONE, NONE, NONE, NONE),
         (0, 33, 25, 46, 33, 34, 31, 25, 11),
         (0, 102, 39, 93, 54, 54, 86, 69, 31),
         (1, NONE, 74265, 7462, 76321, 15429, 13630, 74265, 71181),
         (1, NONE, 15686, NONE, 78120, 76578, NONE, 17742, NONE),
+        (1, NONE, 68097, NONE, NONE, NONE, NONE, NONE, NONE),
         (0, 41, 33, 17, 62, 61, 55, 33, 14),
         (0, 119, 67, 66, 92, 84, 87, 70, 89),
-        (1, 234058, 76321, 72209, 13630, 229175, 231488, 76321, 15961),
-        (1, NONE, 233544, 231488, 227376, NONE, NONE, 221208, 221208),
-        (0, 1, 1, 0, 0, 1, 1, 1, 148),
-        (1, 16714, 68097, 9518, 134228, 15686, 32391, 18256, 8084),
-        (1, 145022, 15943, 136284, NONE, 87372, 134228, 134485, 72723),
-        (1, NONE, 135770, NONE, NONE, 136027, NONE, NONE, 132686),
+        (1, 219152, 76321, 72209, 13630, 225320, 231231, 76321, 15961),
+        (1, NONE, 219152, 227119, 229432, NONE, NONE, 227376, 223264),
+        (0, 2, 2, 1, 1, 2, 2, 2, 147),
+        (1, 16714, 15943, 9518, 134228, 15686, 32391, 18256, 10131),
+        (1, 145022, 135770, 136284, NONE, 87372, 134228, 134485, 72723),
+        (1, NONE, NONE, NONE, NONE, 136027, NONE, NONE, 132686),
         (0, 144, 96, 144, 136, 120, 104, 128, 112),
         (1, 86416, NONE, NONE, NONE, NONE, NONE, NONE, NONE),
         (0, 99, 86, 99, 38, 62, 91, 18, 45),
         (0, 117, 117, 109, 99, 99, 127, 45, 82),
         (1, 142709, 27765, 16971, 7462, 93283, 80176, 72466, 27693),
-        (1, 16971, 5663, 227119, 16971, 11574, 30335, 22368, 72980),
-        (1, 219152, 80176, NONE, 229432, 225320, 231231, 227376, 22296),
-        (1, NONE, 219152, NONE, NONE, NONE, NONE, NONE, 223264),
-        (0, 2, 2, 1, 1, 2, 2, 2, 147),
-        (1, 136027, 136027, 136541, 135770, 134228, 134485, 134742, 10131),
+        (1, 16971, 5663, 233544, 16971, 11574, 30335, 22368, 72980),
+        (1, 233544, 80176, NONE, 231488, 227376, 223264, 229432, 22296),
+        (1, NONE, 221208, NONE, NONE, NONE, NONE, NONE, 225320),
+        (0, 3, 4, 2, 3, 3, 3, 3, 145),
+        (1, 136027, 136027, 136541, 135770, 134228, 134485, 134742, 14225),
         (1, NONE, NONE, NONE, NONE, NONE, NONE, NONE, 132943),
         (0, 96, 104, 88, 144, 128, 120, 135, 90),
         (1, 74080, NONE, NONE, NONE, NONE, NONE, NONE, NONE),
@@ -381,161 +385,156 @@
         (0, 47, 100, 33, 41, 31, 26, 27, 38),
         (1, 9775, NONE, NONE, NONE, NONE, NONE, NONE, NONE),
         (0, 49, 109, 68, 68, 86, 68, 61, 83),
-        (1, 233544, 221208, 76321, 78377, 227376, 74522, 74779, 225320),
-        (1, NONE, NONE, 233544, 231488, NONE, 223264, 229432, NONE),
-        (0, 3, 4, 2, 3, 3, 3, 3, 145),
-        (1, 74851, 16714, 3864, 3864, 82232, 7976, 28536, 14225),
+        (1, 221208, 223264, 76321, 78377, 229432, 74522, 74779, 219666),
+        (1, NONE, NONE, 219152, 233544, NONE, 227376, 231231, NONE),
+        (0, 4, 0, 4, 4, 4, 4, 4, 0),
+        (1, 74851, 16714, 3864, 3864, 82232, 7976, 28536, 16128),
         (1, 24167, 68868, 138083, 136284, 13630, 87886, 80176, 74779),
         (1, 142966, 134742, NONE, NONE, 138083, 134742, 134999, 24095),
         (1, NONE, NONE, NONE, NONE, NONE, NONE, NONE, 155974),
         (0, 104, 112, 96, 96, 118, 128, 111, 120),
         (1, 76136, NONE, NONE, NONE, NONE, NONE, NONE, NONE),
-        (0, 26, 69, 41, 23, 26, 41, 41, 25),
-        (0, 31, 84, 69, 26, 38, 69, 62, 29),
+        (0, 31, 69, 41, 23, 26, 41, 41, 25),
+        (0, 26, 84, 69, 26, 38, 69, 62, 29),
         (1, 75108, 89428, 78377, 74522, 74522, 16971, 82232, 89171),
         (1, 26223, 17228, 28279, 5920, 16971, 89428, 15429, 25894),
-        (1, 221208, 69125, 219152, 233544, 87629, 227376, 231231, 219666),
-        (1, NONE, NONE, NONE, NONE, 229432, NONE, NONE, NONE),
-        (0, 4, NONE, 4, 4, 4, 4, 4, 0),
-        (1, 138854, 223264, 140653, 138083, 134485, 134999, NONE, 156222),
-        (0, 89, 0, 104, 126, 144, 144, 110, 103),
-        (1, 72281, 142709, NONE, NONE, NONE, NONE, NONE, NONE),
-        (0, 34, 120, 23, 31, 41, 23, 49, 21),
-        (0, NONE, NONE, NONE, NONE, 60, 49, 103, 66),
-        (1, 25966, NONE, NONE, NONE, 30335, 17228, 15686, 74265),
-        (1, NONE, NONE, NONE, NONE, 87886, 89685, 88143, 16128),
-        (0, 42, 15, 26, 34, 30, 30, 19, 28),
-        (0, 108, 41, NONE, NONE, 49, 92, 37, 67),
-        (1, 223264, 1808, 74522, 76578, 226862, 229432, 225063, 227376),
-        (0, 5, 23, NONE, NONE, 5, 5, 5, 151),
-        (1, 28279, NONE, 14658, 80176, 9518, 11831, 30592, 23581),
-        (1, 138083, NONE, NONE, 24424, 88143, 91227, 89428, 80176),
-        (0, 112, 49, 34, 61, NONE, NONE, NONE, NONE),
-        (0, NONE, NONE, 108, 108, NONE, NONE, NONE, NONE),
-        (1, 78192, 225320, 76578, 221208, 134742, 136027, NONE, 131401),
-        (1, NONE, NONE, 221208, NONE, NONE, NONE, NONE, NONE),
-        (0, 62, 11, 5, 5, 88, 96, 117, 128),
-        (0, 85, NONE, NONE, NONE, 37, 34, 21, 68),
+        (1, 223264, 69125, 221208, 221208, 87629, 229432, 225063, 227376),
+        (1, NONE, 225320, NONE, NONE, 226862, NONE, NONE, NONE),
+        (0, 5, 11, 5, 5, 5, 5, 5, 151),
+        (0, 39, NONE, NONE, NONE, NONE, NONE, NONE, NONE),
+        (1, 138854, 142709, 140653, 138083, 134485, 134999, NONE, 156222),
+        (0, 89, 120, 104, 126, 144, 144, 110, 103),
+        (1, 72281, NONE, NONE, NONE, NONE, NONE, NONE, NONE),
+        (0, 34, 15, 23, 31, 41, 23, 49, 21),
+        (0, NONE, 41, 26, 34, 60, 49, 103, 66),
+        (1, 25966, 1808, 74522, 76578, 30335, 17228, 15686, 74265),
+        (1, NONE, 70667, 14658, 80176, 87886, 89685, 88143, 1943),
+        (0, 42, 23, NONE, NONE, 30, 30, 19, 28),
+        (0, 108, 49, NONE, NONE, 49, 92, 37, 67),
+        (1, 219409, 227376, NONE, 24424, 233544, 233544, 224806, 223007),
+        (0, 6, 13, 34, 61, 6, 6, 6, 150),
+        (1, 28279, 3864, NONE, NONE, 9518, 11831, 30592, 23581),
+        (1, 138083, 136541, NONE, NONE, 88143, 91227, 89428, 80176),
+        (0, 112, 128, 108, 108, NONE, NONE, NONE, NONE),
+        (1, 78192, NONE, 76578, 228918, 134742, 136027, NONE, 131401),
+        (0, 62, 12, NONE, NONE, 88, 96, 117, 128),
+        (1, NONE, 70924, 223264, NONE, NONE, NONE, NONE, NONE),
+        (0, 85, 62, 9, 6, 37, 34, 21, 68),
         (0, NONE, NONE, NONE, NONE, 92, 38, 127, 81),
-        (1, 71253, 70667, 15172, 11574, 15172, 24424, 32391, 82232),
-        (1, 27765, 3864, 80176, 87629, 89428, 78377, 89685, 1943),
-        (1, 219409, 136541, 142709, 138340, 233544, 233544, 224806, 223007),
-        (0, 6, 128, 112, 112, 6, 6, 6, 150),
-        (1, NONE, NONE, NONE, NONE, NONE, NONE, NONE, 137055),
-        (0, 10, 12, 31, 30, 96, 119, 136, 136),
-        (0, 39, NONE, 42, 42, 42, 42, 22, 33),
-        (1, 138340, 70924, 78634, 78634, NONE, NONE, NONE, NONE),
-        (0, 120, 62, NONE, NONE, 53, 60, 53, 69),
-        (1, 80248, 14915, 15429, 15172, 89685, 80433, 78377, 70667),
-        (1, 5663, 78377, 90970, 87886, 5663, 14915, 13373, 3990),
-        (0, 55, NONE, NONE, NONE, 29, 27, 28, 41),
-        (0, 93, NONE, NONE, NONE, 35, 61, 126, 71),
-        (1, 73309, 227376, 223264, 228918, 219152, 221208, 226605, 229432),
-        (1, 225320, NONE, NONE, NONE, NONE, NONE, NONE, NONE),
-        (0, 38, 13, 9, 6, 7, 7, 7, 149),
-        (1, 7462, NONE, 140396, 140396, 78377, 15172, 26223, 90970),
-        (1, 140653, NONE, NONE, NONE, 28022, 91484, 80433, 6037),
-        (0, 128, 38, 120, 117, 104, 111, 144, 144),
-        (1, 82304, 138340, NONE, NONE, NONE, NONE, NONE, NONE),
-        (0, 57, 135, 49, 29, 57, 35, 29, 26),
-        (0, 87, 26, 61, 43, 66, 45, 118, 87),
-        (1, 7719, 15172, 3607, 78891, 7462, 76578, 72723, 94311),
-        (1, 227376, 80433, NONE, 30078, 80433, 15429, 13630, 231488),
-        (1, NONE, NONE, NONE, 68354, 221208, 227119, 231488, NONE),
-        (0, 9, 34, 50, 37, 9, 9, 9, 2),
-        (0, 11, 65, 62, 85, NONE, NONE, NONE, NONE),
-        (1, 140396, 229432, 225320, 225320, NONE, NONE, NONE, 16642),
-        (0, 97, 3, 18, 19, 135, 126, 88, 135),
-        (1, 74337, 15429, 72466, 91227, NONE, NONE, NONE, NONE),
-        (1, NONE, NONE, 5663, 5663, NONE, NONE, NONE, NONE),
-        (0, 95, NONE, NONE, NONE, 65, 36, 23, 15),
-        (1, 13630, 71181, 80433, NONE, NONE, NONE, NONE, NONE),
-        (0, 13, NONE, 127, 127, 67, 52, 91, 59),
-        (0, 94, NONE, 22, 35, NONE, NONE, NONE, NONE),
-        (1, 229432, 140653, NONE, NONE, 13116, 78634, 91227, 88657),
-        (0, 12, 119, 35, 66, NONE, NONE, NONE, NONE),
-        (0, 105, 42, NONE, NONE, NONE, NONE, NONE, NONE),
-        (1, 76393, NONE, 13373, 91484, 91484, 13116, 25966, NONE),
-        (0, 14, 66, NONE, NONE, 15, 53, 31, 36),
-        (0, 101, NONE, NONE, NONE, 87, 57, 36, 111),
-        (1, 11831, 1551, 80690, 13373, 223264, 225063, 233544, 233544),
-        (1, 221465, 231231, 227376, 226605, NONE, NONE, NONE, NONE),
-        (0, 45, 20, 10, 7, 10, 10, 10, 3),
-        (1, 9261, 72980, NONE, NONE, 78634, 74779, 24167, 16899),
-        (1, NONE, NONE, NONE, NONE, 5406, 13373, NONE, 76321),
-        (0, 20, 127, 135, 135, 111, 103, 119, 127),
-        (0, 63, 7, 30, 49, 23, 65, 66, 37),
-        (0, 113, 50, 43, 67, 93, 66, 92, 60),
-        (1, 78449, 3607, 13630, 5406, 11317, 76835, 91484, 78377),
-        (1, 13887, 74522, 76835, 72723, 76835, 11060, 27765, 231231),
-        (0, 21, 35, 51, 15, NONE, NONE, NONE, 4),
-        (0, 92, 94, 65, 65, NONE, NONE, NONE, NONE),
-        (1, 223521, 227119, 229175, 229175, 231231, 228918, 219152, 17156),
-        (0, 18, 6, 12, 9, 11, 11, 11, 84),
-        (0, 121, NONE, NONE, NONE, 119, 95, 102, 49),
-        (0, NONE, NONE, NONE, NONE, 94, 88, 34, 61),
-        (1, 80505, 76578, 3350, 27765, NONE, NONE, NONE, 74522),
-        (0, 7, NONE, NONE, NONE, 95, 118, 67, 22),
-        (0, 50, NONE, NONE, NONE, NONE, NONE, NONE, 119),
-        (1, 225577, 13630, 78891, 89685, 5149, 11317, 76578, 229175),
-        (0, 54, 103, 126, 119, 45, 37, NONE, 5),
-        (1, NONE, NONE, NONE, NONE, NONE, NONE, 30335, 17413),
-        (0, 15, 43, 52, 86, 100, 93, 46, 85),
-        (0, 98, 102, 67, 110, NONE, NONE, 57, 57),
-        (1, 74594, 78634, 5406, 5149, NONE, NONE, NONE, NONE),
-        (1, NONE, 7462, 80947, 76835, NONE, NONE, NONE, NONE),
-        (0, NONE, NONE, NONE, NONE, NONE, NONE, NONE, 126),
-        (1, NONE, 229175, 231231, 231231, 225063, 223007, 227119, 218124),
-        (0, 58, 9, 13, 10, 18, 18, 12, 6),
-        (1, NONE, NONE, NONE, NONE, NONE, NONE, 11317, 17670),
-        (0, 22, 111, 111, 111, 126, 102, 109, 91),
-        (0, 23, 51, 7, 57, 50, 59, 65, 30),
-        (0, NONE, 101, 57, 87, 59, 94, 95, 52),
-        (1, 227633, 80690, 81204, 7205, NONE, NONE, NONE, NONE),
-        (0, 19, 57, 15, 59, NONE, NONE, NONE, 65),
-        (0, 106, 110, 86, 88, NONE, NONE, NONE, 102),
-        (1, 76650, 223007, 228918, 227119, 227119, 220951, 30078, 218381),
-        (0, 29, 10, 19, 11, 19, 12, NONE, 7),
-        (0, 65, NONE, 110, 118, NONE, NONE, NONE, NONE),
-        (1, 221722, 76835, NONE, NONE, NONE, NONE, 222750, 17927),
-        (0, 46, 87, 58, 60, 103, 110, 13, 92),
-        (0, 66, 99, 87, 93, 58, 22, 93, 34),
-        (0, 114, 108, NONE, NONE, 117, 50, 20, 53),
-        (1, 78706, 78891, 225063, 225063, NONE, NONE, NONE, 219923),
-        (1, NONE, 225063, NONE, NONE, NONE, NONE, NONE, NONE),
-        (0, 35, 18, 20, 12, 22, 58, 58, 97),
-        (1, NONE, NONE, NONE, NONE, NONE, NONE, 28022, 15713),
-        (0, 67, 22, 11, 95, 101, 109, 59, 86),
-        (0, 43, 27, 118, 14, NONE, NONE, 99, 42),
-        (0, NONE, 95, 59, 94, NONE, NONE, NONE, 101),
-        (1, 223778, 80947, NONE, NONE, NONE, NONE, NONE, NONE),
-        (0, 30, 29, 60, 22, NONE, NONE, NONE, 50),
-        (0, 136, 58, 100, 50, NONE, NONE, NONE, 94),
-        (1, NONE, 218895, 224806, 226862, 228918, 222750, 224549, 220180),
-        (0, 68, 19, 21, 18, 12, 13, 14, 98),
-        (1, NONE, NONE, NONE, NONE, NONE, NONE, NONE, 13666),
-        (0, 51, 30, 95, 103, 110, 99, 94, 99),
-        (0, NONE, 59, 6, 52, 43, 28, 60, 58),
-        (0, NONE, NONE, 101, 58, 52, 29, 112, 108),
-        (1, 225834, 220951, 226862, 220951, 223007, 224806, 220437, 218638),
-        (0, 27, 14, 27, 20, 27, 14, 15, 1),
-        (0, 69, 44, 28, 102, 102, 117, 100, 110),
-        (0, 86, 53, 103, 53, 21, 51, 51, 35),
-        (0, 59, 36, 14, 101, 51, 100, 90, 118),
-        (0, 61, 52, 53, 13, 36, 21, 42, 43),
-        (0, 44, 45, 94, 51, 108, 101, 52, 44),
-        (1, 231488, NONE, 220951, 223007, 224806, 221979, 220694, 221979),
-        (0, 28, 46, 37, 27, 13, 15, 101, 23),
-        (0, 70, 60, 102, 109, 109, 108, 43, 93),
-        (0, 52, 21, 29, 21, 20, 43, 50, 51),
-        (0, NONE, NONE, 44, 44, NONE, NONE, NONE, NONE),
-        (1, 218638, NONE, 223007, 222750, NONE, NONE, 222236, NONE),
-        (0, 37, 54, 45, 28, 44, 44, 108, 117),
-        (1, NONE, NONE, 222750, 224549, 222750, 226605, NONE, 224806),
-        (0, 53, 61, 36, 36, 14, 19, 35, 100),
-        (0, 60, 28, NONE, NONE, 28, 20, 44, 109),
-        (1, NONE, NONE, NONE, NONE, 224549, 224292, 222493, 220437),
-        (0, 36, 37, NONE, NONE, NONE, NONE, NONE, NONE),
+        (1, 71253, 14915, 15172, 11574, 15172, 24424, 32391, 82232),
+        (1, 27765, 78377, 80176, 87629, 89428, 78377, 89685, 3990),
+        (1, 225320, 229432, 142709, 138340, 219152, 221208, 226605, 229432),
+        (0, 38, 3, 112, 112, 7, 7, 7, 149),
+        (0, 10, 38, 31, 30, NONE, NONE, NONE, NONE),
+        (0, 55, NONE, 42, 42, NONE, NONE, NONE, NONE),
+        (1, 138340, 138340, 78634, 78634, NONE, NONE, NONE, 137055),
+        (0, 120, 135, NONE, NONE, 96, 119, 136, 136),
+        (0, NONE, 26, NONE, NONE, 42, 42, 22, 33),
+        (0, NONE, NONE, NONE, NONE, 53, 60, 53, 69),
+        (1, 80248, 15172, 15429, 15172, 89685, 80433, 78377, 70667),
+        (1, 5663, 80433, 90970, 87886, 5663, 14915, 13373, 6037),
+        (0, 63, 34, NONE, NONE, 29, 27, 28, 41),
+        (0, 93, 65, NONE, NONE, 35, 61, 126, 71),
+        (1, 73309, 231231, 225320, 225320, 221208, 227119, 231488, 231488),
+        (0, NONE, NONE, NONE, NONE, 9, 9, 9, 2),
+        (1, 227376, NONE, NONE, NONE, 78377, 15172, 26223, 90970),
+        (1, NONE, NONE, NONE, NONE, 28022, 91484, 80433, 16642),
+        (0, 9, 20, 18, 19, 104, 111, 144, 144),
+        (0, NONE, NONE, NONE, NONE, 57, 35, 29, 26),
+        (0, NONE, NONE, NONE, NONE, 66, 45, 118, 87),
+        (1, 7462, 15429, 140396, 140396, 7462, 76578, 72723, 94311),
+        (1, 140653, 71181, NONE, NONE, 80433, 15429, 13630, 233544),
+        (1, NONE, 140653, NONE, NONE, 223264, 225063, 233544, NONE),
+        (0, 128, 119, 120, 117, 10, 10, 10, 3),
+        (1, 82304, NONE, NONE, NONE, NONE, NONE, NONE, 16899),
+        (0, 57, 42, 49, 29, 135, 126, 88, 135),
+        (0, 87, 66, 61, 43, 65, 36, 23, 15),
+        (1, 7719, 1551, 3607, 78891, NONE, NONE, NONE, NONE),
+        (0, NONE, NONE, NONE, NONE, 67, 52, 91, 59),
+        (1, 229432, 72980, 72466, 30078, 13116, 78634, 91227, 88657),
+        (1, NONE, 227119, NONE, 68354, 91484, 13116, 25966, NONE),
+        (0, 12, 6, 50, 37, 15, 53, 31, 36),
+        (0, 11, 127, 62, 85, 87, 57, 36, 111),
+        (1, 140396, NONE, 227376, 226605, 231231, 228918, 219152, 231231),
+        (0, 97, 7, 10, 7, 11, 11, 11, 4),
+        (1, 74337, NONE, 5663, 91227, 78634, 74779, 24167, 17156),
+        (1, NONE, NONE, 80433, 5663, 5406, 13373, NONE, 76321),
+        (0, 95, 50, 127, 127, 111, 103, 119, 127),
+        (1, 13630, 3607, NONE, NONE, NONE, NONE, NONE, NONE),
+        (0, 13, NONE, 22, 35, 23, 65, 66, 37),
+        (0, 94, NONE, 35, 66, 93, 66, 92, 60),
+        (1, 221465, 74522, 13373, 91484, 11317, 76835, 91484, 78377),
+        (1, NONE, NONE, 80690, 13373, 76835, 11060, 27765, 229175),
+        (1, NONE, NONE, 229175, 229175, 225063, 223007, NONE, NONE),
+        (0, 45, 35, 12, 9, 18, 18, NONE, 5),
+        (1, 9261, NONE, NONE, NONE, NONE, NONE, 227119, 17413),
+        (0, 105, 94, 135, 135, 119, 95, 12, 84),
+        (1, 76393, 229175, NONE, NONE, NONE, NONE, NONE, NONE),
+        (0, 14, 9, 30, 49, 94, 88, 102, 49),
+        (0, 101, NONE, 43, 67, 95, 118, 34, 61),
+        (1, 11831, 76578, 13630, 5406, 5149, 11317, NONE, 74522),
+        (1, 223521, 13630, 76835, 72723, NONE, NONE, NONE, NONE),
+        (0, 18, 103, 51, 15, 45, 37, 67, 22),
+        (0, 7, 43, 65, 65, 100, 93, NONE, 119),
+        (0, 20, 102, NONE, NONE, NONE, NONE, NONE, NONE),
+        (1, NONE, 78634, 231231, 231231, 227119, 220951, 76578, 218124),
+        (0, 113, NONE, 13, 10, 19, 12, NONE, 6),
+        (1, 78449, 7462, 3350, 27765, NONE, NONE, 30335, 17670),
+        (1, 13887, 223007, 78891, 89685, NONE, NONE, NONE, NONE),
+        (0, 21, 10, 126, 119, 126, 102, 46, 85),
+        (0, 92, 111, 52, 86, 50, 59, 57, 57),
+        (0, NONE, NONE, 67, 110, 59, 94, NONE, 126),
+        (1, 225577, NONE, 5406, 5149, 228918, 222750, 222750, 218381),
+        (1, NONE, NONE, 80947, 76835, NONE, NONE, NONE, NONE),
+        (0, 54, 51, NONE, NONE, 12, 13, 13, 7),
+        (0, 121, 101, NONE, NONE, NONE, NONE, NONE, NONE),
+        (1, 80505, 80690, 228918, 227119, NONE, NONE, 11317, 17927),
+        (0, 15, 57, 19, 11, 103, 110, 109, 91),
+        (0, 50, 110, 111, 111, 58, 22, 65, 30),
+        (1, 227633, 225063, NONE, NONE, NONE, NONE, NONE, NONE),
+        (0, 19, 18, 7, 57, 117, 50, 95, 52),
+        (0, 23, NONE, 57, 87, 22, 58, NONE, 65),
+        (0, 98, NONE, NONE, NONE, 101, 109, NONE, 102),
+        (1, 74594, 76835, 81204, 7205, 223007, 224806, 30078, 219923),
+        (0, 58, 87, 15, 59, 27, 14, NONE, 97),
+        (0, 22, 99, 86, 88, NONE, NONE, NONE, NONE),
+        (0, 65, 108, NONE, NONE, NONE, NONE, NONE, NONE),
+        (1, 221722, 78891, 225063, 225063, NONE, NONE, 224549, 15713),
+        (0, 46, NONE, 20, 12, 110, 99, 14, 92),
+        (0, 106, NONE, 110, 118, 43, 28, 93, 34),
+        (1, 76650, 218895, NONE, NONE, NONE, NONE, NONE, NONE),
+        (0, 29, 19, 58, 60, 52, 29, 20, 53),
+        (0, 66, 22, 87, 93, NONE, NONE, NONE, NONE),
+        (1, 223778, NONE, 224806, 226862, 224806, 221979, NONE, 220180),
+        (0, 30, 27, 21, 18, 13, 15, 58, 98),
+        (1, NONE, NONE, NONE, NONE, NONE, NONE, 28022, 13666),
+        (0, 67, 95, 11, 95, 102, 117, 59, 86),
+        (0, 114, NONE, 118, 14, 21, 51, 99, 42),
+        (1, 78706, 80947, NONE, NONE, NONE, NONE, NONE, NONE),
+        (0, 35, 29, 59, 94, 51, 100, NONE, 101),
+        (0, 68, 58, 60, 22, 36, 21, NONE, 50),
+        (0, 43, NONE, 100, 50, 108, 101, NONE, 94),
+        (1, 225834, 220951, 226862, 220951, 222750, 226605, 220437, 218638),
+        (0, 27, 14, 27, 20, 14, 19, 15, 1),
+        (0, 136, 30, 95, 103, 109, 108, 94, 99),
+        (0, 69, 59, 6, 52, 20, 43, 60, 58),
+        (0, 51, 45, 101, 58, 44, 44, 112, 108),
+        (1, 231488, NONE, 220951, 223007, 224549, 224292, 220694, 221979),
+        (0, 28, 44, 37, 27, 28, 20, 100, 23),
+        (0, 61, 53, 28, 102, NONE, NONE, 51, 110),
+        (0, 86, 36, 103, 53, NONE, NONE, 90, 35),
+        (0, 59, 52, 14, 101, NONE, NONE, 42, 118),
+        (0, 53, 21, 53, 13, NONE, NONE, 52, 43),
+        (0, 44, 46, 94, 51, NONE, NONE, NONE, 44),
+        (1, 218638, NONE, 223007, 222750, NONE, NONE, 222236, 224806),
+        (0, 37, 60, 45, 28, NONE, NONE, 101, 93),
+        (0, 70, 28, 102, 109, NONE, NONE, 43, 51),
+        (0, 52, 54, 29, 21, NONE, NONE, 50, 117),
+        (0, 36, 61, 44, 44, NONE, NONE, NONE, NONE),
+        (1, NONE, NONE, 222750, 224549, NONE, NONE, 222493, 220437),
+        (0, 60, 37, 36, 36, NONE, NONE, 108, 100),
+        (0, NONE, NONE, NONE, NONE, NONE, NONE, 35, 109),
+        (0, NONE, NONE, NONE, NONE, NONE, NONE, 44, NONE),
         (1, NONE, NONE, NONE, NONE, NONE, NONE, 224292, 222236),
     ),
 )
@@ -596,6 +595,8 @@
             upper[slot] = block.T
             flipped[slot] = block
 
+    for d in range(HALF):
+        flipped[OWN + d] = upper[OWN + d].T
     pl.semaphore_wait(barrier, 3)
     pl.semaphore_signal(entered, inc=1, device_id=peers[2], device_id_type=MESH)
 
@@ -655,9 +656,6 @@
         pl.when(ring == n)(functools.partial(exchange, events))
         counts = [sum(e[0] == 1 and e[1 + y] != NONE for e in events) for y in range(RING)]
         sends = jnp.where(ring == n, pick([jnp.int32(c) for c in counts]), sends)
-    for d in range(HALF):
-        flipped[OWN + d] = upper[OWN + d].T
-
     def block_at(k, j):
         if abs(k - j) > BAND:
             return jnp.zeros((size, size), upper.dtype)

time: 39.3 us -> 38.9 us (0.990); the launches traced: 38.8 us -> 38.8 us
  no operation moved by 1% of the time
where the time goes in v4:
time: 38.9 us; the launch traced here: 38.8 us
  Pallas kernels  38 us (98%)
  local copies, waits for them, and re-layouts  0.8 us (2%)
    pallas_call x1, Pallas kernels, per_device(): pl.pallas_call(kernel, out_shape=jax.ShapeDtypeStruct(blocks.shape, kind)...  38 us
    unnamed x1, local copies, waits for them, and re-layouts  0.8 us

profile of v4, /device:TPU:6, one launch (start us, length us, event | category | flops | bytes accessed | tf_op | source)
XLA Modules:
  0.0 38.8 jit_solution(11826549155000751610)
XLA Ops:
  0.0 38.0 %purify.1 = bf16[1,16,128,128]{3,2,1,0:T(8,128)(2,1)S(1)} custom-call(s32[1,16]{1,0:T(1,128)} %cols_hbm.1, bf16[1,16,128,128]{3,2,1,0:T(8,128)(2,1)} %blocks_hbm.1), custom_call_target="tpu_custom_call" | custom-call | flops 1820327936 | bytes 2097152 | tf_op jit(solution)/shard_map/purify/pallas_call | solution.py:700
  38.0 0.8 %copy.4 = bf16[1,16,128,128]{3,2,1,0:T(8,128)(2,1)} copy(bf16[1,16,128,128]{3,2,1,0:T(8,128)(2,1)S(1)} %purify.1) | data formatting | bytes 1048576

commit v5 on v4

--- a/solution.py
+++ b/solution.py
@@ -545,7 +545,7 @@
     return row // cols, lax.rem(row, cols)
 
 
-def kernel(cols_hbm, blocks_hbm, out_ref, cols_ref, blocks_ref, own, square, upper, flipped, newband, in_sem, entered, send_sem, recv_sem):
+def kernel(cols_hbm, blocks_hbm, out_ref, cols_ref, blocks_ref, own, square, upper, flipped, in_sem, entered, send_sem, recv_sem):
     size = blocks_ref.shape[-1]
     loads = [
         pltpu.make_async_copy(cols_hbm, cols_ref, in_sem.at[0]),
@@ -685,9 +685,11 @@
         for w in range(width):
             part = slice((first + w) * size, (first + w + 1) * size)
             value = 3.0 * square[:, part].astype(jnp.float32) - 2.0 * total[:, w * size : (w + 1) * size]
-            newband[first + w] = value.astype(newband.dtype)
-    for s in range(WINDOW - 1):
-        out_ref[0, s] = jnp.where(s < missing, newband[s], newband[s + 1])
+            value = value.astype(out_ref.dtype)
+            s = first + w - 1
+            if s >= 0:
+                out_ref[0, s] = jnp.where(s < missing, before, value)
+            before = value
 
     for number in sorted({sum(e[0] == 1 and e[1 + y] != NONE for e in events) for events in EVENTS for y in range(RING)}):
         blocks = upper.at[pl.ds(0, number)]
@@ -709,7 +711,6 @@
             pltpu.VMEM((size, WINDOW * size), kind),
             pltpu.VMEM((WINDOW * HALF, size, size), kind),
             pltpu.VMEM((WINDOW * HALF, size, size), kind),
-            pltpu.VMEM((WINDOW, size, size), kind),
             pltpu.SemaphoreType.DMA((2,)),
             pltpu.SemaphoreType.REGULAR,
             pltpu.SemaphoreType.DMA,

time: 38.9 us -> 38.8 us (level)
  no operation moved by 1% of the time
where the time goes in v5:
time: 38.8 us; the launch traced here: 38.7 us
  Pallas kernels  37.9 us (98%)
  local copies, waits for them, and re-layouts  0.8 us (2%)
    pallas_call x1, Pallas kernels, per_device(): pl.pallas_call(kernel, out_shape=jax.ShapeDtypeStruct(blocks.shape, kind)...  37.9 us
    unnamed x1, local copies, waits for them, and re-layouts  0.8 us

profile of v5, /device:TPU:6, one launch (start us, length us, event | category | flops | bytes accessed | tf_op | source)
XLA Modules:
  0.0 38.7 jit_solution(6184829306409153657)
XLA Ops:
  0.0 37.9 %purify.1 = bf16[1,16,128,128]{3,2,1,0:T(8,128)(2,1)S(1)} custom-call(s32[1,16]{1,0:T(1,128)} %cols_hbm.1, bf16[1,16,128,128]{3,2,1,0:T(8,128)(2,1)} %blocks_hbm.1), custom_call_target="tpu_custom_call" | custom-call | flops 1820327936 | bytes 2097152 | tf_op jit(solution)/shard_map/purify/pallas_call | solution.py:702
  37.9 0.8 %copy.4 = bf16[1,16,128,128]{3,2,1,0:T(8,128)(2,1)} copy(bf16[1,16,128,128]{3,2,1,0:T(8,128)(2,1)S(1)} %purify.1) | data formatting | bytes 1048576
